TPU v7x, 256 devices: a whole 4x4x8 slice. The times are simulated.
256 devices in a mesh: loop: 32 (over x, z), group: 8 (over y, core).
Axes of the slice: x: 4, y: 4, z: 8, core: 2. Of those that a mesh axis runs over, the one named last changes fastest.
Arguments:
- features: bfloat16 [6144, 256], P(('loop', 'group')), may hold values from -6 to 6
- scale_exponents: int32 [8], replicated, may hold values from -1 to 2
- targets: int32 [6144], P(('loop', 'group')), may hold values from 0 to 262143
- centres: bfloat16 [262144, 256], P(('loop', 'group')), may hold values from -1 to 1
Outputs:
- row_loss: float32 [6144], P(('loop', 'group'))
- feature_grad: float32 [6144, 256], P(('loop', 'group'))
All inputs are finite; a program needn't handle non-finite values.
Results may differ from a plain program's by a relative error of at most 0.015.
Values may be sent and summed in bfloat16 or wider, within the bound.
A program may use at most 192 MiB of HBM per device.

v0:
```python
import jax
import jax.numpy as jnp
from jax import lax
from jax.sharding import PartitionSpec as P

QB = 32


def from_behind(value, axis, steps):
    count = lax.axis_size(axis)
    pairs = [(source, (source + steps) % count) for source in range(count)]
    return lax.ppermute(value, axis, pairs)


def merged(array, axis, combine):
    everything = jax.tree.map(lambda part: lax.all_gather(part, axis), array)
    initial = jax.tree.map(lambda part: part[0], everything)

    def lap(k, so_far):
        return combine(so_far, jax.tree.map(lambda part: part[k], everything))

    return lax.fori_loop(1, lax.axis_size(axis), lap, initial)


def visit_shard(block_rows, label_ids, state, centres, first_class):
    running_max, exp_total, accum, target_rows, target_logit = state
    shard_rows = centres.shape[0]
    logits = lax.dot_general(
        block_rows, centres, (((1,), (1,)), ((), ())), preferred_element_type=jnp.float32
    )
    new_max = jnp.maximum(running_max, jnp.max(logits, axis=1))
    rescale = jnp.exp(running_max - new_max)
    weights = jnp.exp(logits - new_max[:, None])
    exp_total = exp_total * rescale + jnp.sum(weights, axis=1)
    accum = accum * rescale[:, None] + jnp.dot(
        weights.astype(jnp.bfloat16), centres, preferred_element_type=jnp.float32
    )
    local_ids = label_ids - first_class
    in_shard = (local_ids >= 0) & (local_ids < shard_rows)
    picked = jnp.take(centres, jnp.clip(local_ids, 0, shard_rows - 1), axis=0)
    target_hits = jnp.where(in_shard[:, None], picked, jnp.zeros_like(picked))
    target_rows = target_rows + target_hits
    target_logit = target_logit + jnp.sum(
        block_rows.astype(jnp.float32) * target_hits.astype(jnp.float32), axis=1
    )
    return (new_max, exp_total, accum, target_rows, target_logit)


def merge_stats(left_stats, right_stats):
    new_max = jnp.maximum(left_stats[0], right_stats[0])
    new_total = left_stats[1] * jnp.exp(left_stats[0] - new_max) + right_stats[1] * jnp.exp(
        right_stats[0] - new_max
    )
    return (new_max, new_total, left_stats[2] + right_stats[2])


def start_state(row_count, width, target_type):
    return (
        jnp.full((row_count,), -jnp.inf, jnp.float32),
        jnp.zeros((row_count,), jnp.float32),
        jnp.zeros((row_count, width), jnp.float32),
        jnp.zeros((row_count, width), target_type),
        jnp.zeros((row_count,), jnp.float32),
    )


def body(features, scale_exponents, targets, centres):
    loop_size = lax.axis_size("loop")
    group_size = lax.axis_size("group")
    loop_index = lax.axis_index("loop")
    group_index = lax.axis_index("group")
    width = features.shape[1]
    quant_scale = jnp.repeat(jnp.exp2(scale_exponents.astype(jnp.float32)), QB)
    squashed = jnp.tanh(features.astype(jnp.float32) / quant_scale)
    student = (quant_scale * squashed).astype(jnp.bfloat16)
    block_rows, block_ids = (
        lax.all_gather(student, "group", axis=0, tiled=True),
        lax.all_gather(targets, "group", axis=0, tiled=True),
    )
    first_class = (loop_index * group_size + group_index) * centres.shape[0]
    own_count = features.shape[0]
    block_count = block_rows.shape[0]

    def cycle_turn(turn_index, carried):
        state = visit_shard(carried[0], carried[1], carried[2:], centres, first_class)
        return (
            from_behind(carried[0].astype(jnp.float32), "loop", 1).astype(jnp.bfloat16),
            from_behind(carried[1], "loop", 1),
            from_behind(state[0], "loop", 1),
            from_behind(state[1], "loop", 1),
            from_behind(state[2], "loop", 1),
            from_behind(state[3].astype(jnp.float32), "loop", 1).astype(jnp.bfloat16),
            from_behind(state[4], "loop", 1),
        )

    finished = lax.fori_loop(
        0,
        loop_size,
        cycle_turn,
        (block_rows, block_ids) + start_state(block_count, width, jnp.bfloat16),
    )
    running_max, exp_total, accum, target_rows, target_logit = finished[2:]
    target_sum = target_rows.astype(jnp.float32)
    top_max, top_total, top_logit = merged(
        (running_max, exp_total, target_logit), "group", merge_stats
    )
    rescale_share = jnp.exp(running_max - top_max) / top_total
    partial_grad = accum * rescale_share[:, None] - target_sum
    own_grad = lax.psum_scatter(
        partial_grad.astype(jnp.bfloat16), "group", scatter_dimension=0, tiled=True
    ).astype(jnp.float32)
    own_offset = group_index * own_count
    own_max = lax.dynamic_slice_in_dim(top_max, own_offset, own_count, 0)
    own_total = lax.dynamic_slice_in_dim(top_total, own_offset, own_count, 0)
    own_logit = lax.dynamic_slice_in_dim(top_logit, own_offset, own_count, 0)
    row_loss = own_max + jnp.log(own_total) - own_logit
    feature_grad = own_grad * (1.0 - squashed * squashed)
    return (row_loss, feature_grad)


def solution(mesh):
    placed = (P(("loop", "group"), None), P(), P(("loop", "group")), P(("loop", "group"), None))
    return jax.shard_map(
        body,
        mesh=mesh,
        in_specs=placed,
        out_specs=(P(("loop", "group")), P(("loop", "group"), None)),
        check_vma=False,
    )
```

profile of v0, /device:TPU:1, one launch (start us, length us, event | category | flops | bytes accessed | tf_op | source)
XLA Modules:
  0.0 724.2 jit_solution(13516822310121322715)
XLA Ops:
  9.4 8.9 %all-reduce = s32[192]{0:T(256)S(1)} all-reduce(s32[192]{0:T(256)S(1)} %dynamic-update-slice), channel_id=1, replica_groups=mesh['loop'=32,'group'=8] {'group'}, use_global_device_ids=true, to_apply=%add | all-reduce | flops 192 | bytes 1536
  18.5 14.8 %all_gather.24 = bf16[192,256]{1,0:T(8,128)(2,1)S(1)} all-gather(bf16[24,256]{1,0:T(8,128)(2,1)S(1)} %multiply_convert_fusion), channel_id=1, replica_groups=mesh['loop'=32,'group'=8] {'group'}, dimensions={0}, use_global_device_ids=true | all-gather | bytes 110592 | tf_op jit(solution)/shard_map/all_gather | solution.py:77
  34.0 565.2 %while.43 = (s32[]{:T(128)}, bf16[192,256]{1,0:T(8,128)(2,1)S(1)}, s32[192]{0:T(256)S(1)}, f32[192]{0:T(256)S(1)}, f32[192]{0:T(256)S(1)}, /*index=5*/f32[192,25...) while((s32[]{:T(128)}, bf16[192,256]{1,0:T(8,128)(2,1)S(1)}, ...), condition=%wide.region_4.5_spmd.clone, body=%wide.region_0.4_spmd.clone.sunk | while | flops 202902976 | bytes 8492087 | solution.py:96
  60.7 6.9 collective-permute-done.3
  67.7 5.7 collective-permute-done.6
  78.2 6.3 collective-permute-done.3
  84.5 6.1 collective-permute-done.6
  95.2 6.3 collective-permute-done.3
  101.5 6.0 collective-permute-done.6
  112.3 6.3 collective-permute-done.3
  118.6 5.8 collective-permute-done.6
  129.1 6.3 collective-permute-done.3
  135.4 5.7 collective-permute-done.6
  145.9 6.3 collective-permute-done.3
  152.2 5.7 collective-permute-done.6
  162.6 7.4 %collective-permute-done.3 = f32[192]{0:T(256)S(1)} collective-permute-done((f32[192]{0:T(256)S(1)}, f32[192]{0:T(256)S(1)}, u32[]{:S(2)}, u32[]{:S(2)}) %collective-permute-start.3) | collective-permute-done | bytes 800 | tf_op jit(solution)/shard_map/while/body/eval_jaxpr/ppermute | solution.py:12
  170.1 5.7 collective-permute-done.6
  180.5 8.6 %collective-permute-done.3 = f32[192]{0:T(256)S(1)} collective-permute-done((f32[192]{0:T(256)S(1)}, f32[192]{0:T(256)S(1)}, u32[]{:S(2)}, u32[]{:S(2)}) %collective-permute-start.3) | collective-permute-done | bytes 800 | tf_op jit(solution)/shard_map/while/body/eval_jaxpr/ppermute | solution.py:12
  189.2 5.7 collective-permute-done.6
  199.7 8.4 %collective-permute-done.3 = f32[192]{0:T(256)S(1)} collective-permute-done((f32[192]{0:T(256)S(1)}, f32[192]{0:T(256)S(1)}, u32[]{:S(2)}, u32[]{:S(2)}) %collective-permute-start.3) | collective-permute-done | bytes 800 | tf_op jit(solution)/shard_map/while/body/eval_jaxpr/ppermute | solution.py:12
  218.5 7.4 %collective-permute-done.3 = f32[192]{0:T(256)S(1)} collective-permute-done((f32[192]{0:T(256)S(1)}, f32[192]{0:T(256)S(1)}, u32[]{:S(2)}, u32[]{:S(2)}) %collective-permute-start.3) | collective-permute-done | bytes 800 | tf_op jit(solution)/shard_map/while/body/eval_jaxpr/ppermute | solution.py:12
  226.0 5.7 collective-permute-done.6
  236.4 6.3 collective-permute-done.3
  242.7 6.1 collective-permute-done.6
  253.5 6.3 collective-permute-done.3
  259.8 6.0 collective-permute-done.6
  270.5 6.3 collective-permute-done.3
  276.8 5.8 collective-permute-done.6
  287.4 6.3 collective-permute-done.3
  293.7 5.7 collective-permute-done.6
  304.1 6.3 collective-permute-done.3
  310.5 5.7 collective-permute-done.6
  320.9 7.4 %collective-permute-done.3 = f32[192]{0:T(256)S(1)} collective-permute-done((f32[192]{0:T(256)S(1)}, f32[192]{0:T(256)S(1)}, u32[]{:S(2)}, u32[]{:S(2)}) %collective-permute-start.3) | collective-permute-done | bytes 800 | tf_op jit(solution)/shard_map/while/body/eval_jaxpr/ppermute | solution.py:12
  338.8 8.6 %collective-permute-done.3 = f32[192]{0:T(256)S(1)} collective-permute-done((f32[192]{0:T(256)S(1)}, f32[192]{0:T(256)S(1)}, u32[]{:S(2)}, u32[]{:S(2)}) %collective-permute-start.3) | collective-permute-done | bytes 800 | tf_op jit(solution)/shard_map/while/body/eval_jaxpr/ppermute | solution.py:12
  347.4 5.7 collective-permute-done.6
  357.9 8.4 %collective-permute-done.3 = f32[192]{0:T(256)S(1)} collective-permute-done((f32[192]{0:T(256)S(1)}, f32[192]{0:T(256)S(1)}, u32[]{:S(2)}, u32[]{:S(2)}) %collective-permute-start.3) | collective-permute-done | bytes 800 | tf_op jit(solution)/shard_map/while/body/eval_jaxpr/ppermute | solution.py:12
  366.3 5.7 collective-permute-done.6
  376.8 7.4 %collective-permute-done.3 = f32[192]{0:T(256)S(1)} collective-permute-done((f32[192]{0:T(256)S(1)}, f32[192]{0:T(256)S(1)}, u32[]{:S(2)}, u32[]{:S(2)}) %collective-permute-start.3) | collective-permute-done | bytes 800 | tf_op jit(solution)/shard_map/while/body/eval_jaxpr/ppermute | solution.py:12
  384.2 5.7 collective-permute-done.6
  394.7 6.3 collective-permute-done.3
  401.0 6.1 collective-permute-done.6
  411.8 6.3 collective-permute-done.3
  418.1 6.0 collective-permute-done.6
  428.8 6.3 collective-permute-done.3
  435.1 5.8 collective-permute-done.6
  445.6 6.3 collective-permute-done.3
  451.9 5.7 collective-permute-done.6
  462.4 6.3 collective-permute-done.3
  468.7 5.7 collective-permute-done.6
  479.2 7.4 %collective-permute-done.3 = f32[192]{0:T(256)S(1)} collective-permute-done((f32[192]{0:T(256)S(1)}, f32[192]{0:T(256)S(1)}, u32[]{:S(2)}, u32[]{:S(2)}) %collective-permute-start.3) | collective-permute-done | bytes 800 | tf_op jit(solution)/shard_map/while/body/eval_jaxpr/ppermute | solution.py:12
  497.0 8.6 %collective-permute-done.3 = f32[192]{0:T(256)S(1)} collective-permute-done((f32[192]{0:T(256)S(1)}, f32[192]{0:T(256)S(1)}, u32[]{:S(2)}, u32[]{:S(2)}) %collective-permute-start.3) | collective-permute-done | bytes 800 | tf_op jit(solution)/shard_map/while/body/eval_jaxpr/ppermute | solution.py:12
  505.7 5.7 collective-permute-done.6
  516.1 8.4 %collective-permute-done.3 = f32[192]{0:T(256)S(1)} collective-permute-done((f32[192]{0:T(256)S(1)}, f32[192]{0:T(256)S(1)}, u32[]{:S(2)}, u32[]{:S(2)}) %collective-permute-start.3) | collective-permute-done | bytes 800 | tf_op jit(solution)/shard_map/while/body/eval_jaxpr/ppermute | solution.py:12
  524.6 5.7 collective-permute-done.6
  535.0 7.4 %collective-permute-done.3 = f32[192]{0:T(256)S(1)} collective-permute-done((f32[192]{0:T(256)S(1)}, f32[192]{0:T(256)S(1)}, u32[]{:S(2)}, u32[]{:S(2)}) %collective-permute-start.3) | collective-permute-done | bytes 800 | tf_op jit(solution)/shard_map/while/body/eval_jaxpr/ppermute | solution.py:12
  542.5 5.7 collective-permute-done.6
  552.9 6.3 collective-permute-done.3
  559.2 6.1 collective-permute-done.6
  570.0 6.3 collective-permute-done.3
  576.3 6.0 collective-permute-done.6
  587.0 6.3 collective-permute-done.3
  593.3 5.8 collective-permute-done.6
  600.0 88.2 %all-reduce.4 = (f32[1536]{0:T(1024)S(1)}, f32[1536]{0:T(1024)S(1)}, f32[1536]{0:T(1024)S(1)}) all-reduce(f32[1536]{0:T(1024)S(1)} %dynamic-update-slice.1, f32[1536]{0:T(1024)S(1)} %dynamic-update-slice.2, f32[1536]{0:T(1024)S(1)} %dynamic-update-slice.3), channel_id=2, replica_groups=mesh['loop'=32,'group'=8] {'group'}, use_global_device_ids=true, to_apply=%add.1 | all-reduce | flops 4608 | bytes 36864
  690.3 25.6 %reduce-scatter.2.cloned.1.call-done = bf16[24,256]{1,0:T(8,128)(2,1)} async-done(((bf16[192,256]{1,0:T(8,128)(2,1)}), bf16[24,256]{1,0:T(8,128)(2,1)}) %reduce-scatter.2.cloned.1.call-update) | async-done | bytes 12304 | tf_op jit(solution)/shard_map/reduce_scatter | solution.py:109
  (968 shorter events, 188.1 us)
Async XLA Ops:
  7.2 708.8 %reduce-scatter.2.cloned.1.call-start = ((), (), s32[]{:S(2)}) async-start(), calls=%async_computation.1 | async-start | bytes 110592 | tf_op jit(solution)/shard_map/reduce_scatter | solution.py:109
  34.0 21.3 %collective-permute-start = (bf16[192,256]{1,0:T(8,128)(2,1)S(1)}, bf16[192,256]{1,0:T(8,128)(2,1)S(1)}, u32[]{:S(2)}, u32[]{:S(2)}) collective-permute-start(bf16[192,256]{1,0:T(8,128)(2,1)S(1)} %copy.16), channel_id=1, source_target_pairs={{0,8},{8,16},{16,24},{24,32},{32,40},{40,48},{48,56},{56,64},{64,7... | collective-permute-start | bytes 294920 | tf_op jit(solution)/shard_map/while/body/eval_jaxpr/ppermute | solution.py:12
  39.6 15.7 %collective-permute-start.4 = (f32[192,256]{1,0:T(8,128)S(1)}, f32[192,256]{1,0:T(8,128)S(1)}, u32[]{:S(2)}, u32[]{:S(2)}) collective-permute-start(f32[192,256]{1,0:T(8,128)S(1)} %convolution_add_fusion.2), channel_id=1, source_target_pairs={{0,8},{8,16},{16,24},{24,32},{32,40},{40,48},{48,56},{56,64},{64,7... | collective-permute-start | bytes 589832 | tf_op jit(solution)/shard_map/while/body/eval_jaxpr/ppermute | solution.py:12
  55.4 18.1 %collective-permute-start = (bf16[192,256]{1,0:T(8,128)(2,1)S(1)}, bf16[192,256]{1,0:T(8,128)(2,1)S(1)}, u32[]{:S(2)}, u32[]{:S(2)}) collective-permute-start(bf16[192,256]{1,0:T(8,128)(2,1)S(1)} %copy.16), channel_id=1, source_target_pairs={{0,8},{8,16},{16,24},{24,32},{32,40},{40,48},{48,56},{56,64},{64,7... | collective-permute-start | bytes 294920 | tf_op jit(solution)/shard_map/while/body/eval_jaxpr/ppermute | solution.py:12
  58.3 15.2 %collective-permute-start.4 = (f32[192,256]{1,0:T(8,128)S(1)}, f32[192,256]{1,0:T(8,128)S(1)}, u32[]{:S(2)}, u32[]{:S(2)}) collective-permute-start(f32[192,256]{1,0:T(8,128)S(1)} %convolution_add_fusion.2), channel_id=1, source_target_pairs={{0,8},{8,16},{16,24},{24,32},{32,40},{40,48},{48,56},{56,64},{64,7... | collective-permute-start | bytes 589832 | tf_op jit(solution)/shard_map/while/body/eval_jaxpr/ppermute | solution.py:12
  73.5 17.1 %collective-permute-start = (bf16[192,256]{1,0:T(8,128)(2,1)S(1)}, bf16[192,256]{1,0:T(8,128)(2,1)S(1)}, u32[]{:S(2)}, u32[]{:S(2)}) collective-permute-start(bf16[192,256]{1,0:T(8,128)(2,1)S(1)} %copy.16), channel_id=1, source_target_pairs={{0,8},{8,16},{16,24},{24,32},{32,40},{40,48},{48,56},{56,64},{64,7... | collective-permute-start | bytes 294920 | tf_op jit(solution)/shard_map/while/body/eval_jaxpr/ppermute | solution.py:12
  76.5 14.1 %collective-permute-start.4 = (f32[192,256]{1,0:T(8,128)S(1)}, f32[192,256]{1,0:T(8,128)S(1)}, u32[]{:S(2)}, u32[]{:S(2)}) collective-permute-start(f32[192,256]{1,0:T(8,128)S(1)} %convolution_add_fusion.2), channel_id=1, source_target_pairs={{0,8},{8,16},{16,24},{24,32},{32,40},{40,48},{48,56},{56,64},{64,7... | collective-permute-start | bytes 589832 | tf_op jit(solution)/shard_map/while/body/eval_jaxpr/ppermute | solution.py:12
  90.6 17.0 %collective-permute-start = (bf16[192,256]{1,0:T(8,128)(2,1)S(1)}, bf16[192,256]{1,0:T(8,128)(2,1)S(1)}, u32[]{:S(2)}, u32[]{:S(2)}) collective-permute-start(bf16[192,256]{1,0:T(8,128)(2,1)S(1)} %copy.16), channel_id=1, source_target_pairs={{0,8},{8,16},{16,24},{24,32},{32,40},{40,48},{48,56},{56,64},{64,7... | collective-permute-start | bytes 294920 | tf_op jit(solution)/shard_map/while/body/eval_jaxpr/ppermute | solution.py:12
  93.5 14.0 %collective-permute-start.4 = (f32[192,256]{1,0:T(8,128)S(1)}, f32[192,256]{1,0:T(8,128)S(1)}, u32[]{:S(2)}, u32[]{:S(2)}) collective-permute-start(f32[192,256]{1,0:T(8,128)S(1)} %convolution_add_fusion.2), channel_id=1, source_target_pairs={{0,8},{8,16},{16,24},{24,32},{32,40},{40,48},{48,56},{56,64},{64,7... | collective-permute-start | bytes 589832 | tf_op jit(solution)/shard_map/while/body/eval_jaxpr/ppermute | solution.py:12
  107.6 16.8 %collective-permute-start = (bf16[192,256]{1,0:T(8,128)(2,1)S(1)}, bf16[192,256]{1,0:T(8,128)(2,1)S(1)}, u32[]{:S(2)}, u32[]{:S(2)}) collective-permute-start(bf16[192,256]{1,0:T(8,128)(2,1)S(1)} %copy.16), channel_id=1, source_target_pairs={{0,8},{8,16},{16,24},{24,32},{32,40},{40,48},{48,56},{56,64},{64,7... | collective-permute-start | bytes 294920 | tf_op jit(solution)/shard_map/while/body/eval_jaxpr/ppermute | solution.py:12
  110.6 13.8 %collective-permute-start.4 = (f32[192,256]{1,0:T(8,128)S(1)}, f32[192,256]{1,0:T(8,128)S(1)}, u32[]{:S(2)}, u32[]{:S(2)}) collective-permute-start(f32[192,256]{1,0:T(8,128)S(1)} %convolution_add_fusion.2), channel_id=1, source_target_pairs={{0,8},{8,16},{16,24},{24,32},{32,40},{40,48},{48,56},{56,64},{64,7... | collective-permute-start | bytes 589832 | tf_op jit(solution)/shard_map/while/body/eval_jaxpr/ppermute | solution.py:12
  124.5 16.8 %collective-permute-start = (bf16[192,256]{1,0:T(8,128)(2,1)S(1)}, bf16[192,256]{1,0:T(8,128)(2,1)S(1)}, u32[]{:S(2)}, u32[]{:S(2)}) collective-permute-start(bf16[192,256]{1,0:T(8,128)(2,1)S(1)} %copy.16), channel_id=1, source_target_pairs={{0,8},{8,16},{16,24},{24,32},{32,40},{40,48},{48,56},{56,64},{64,7... | collective-permute-start | bytes 294920 | tf_op jit(solution)/shard_map/while/body/eval_jaxpr/ppermute | solution.py:12
  141.3 16.7 %collective-permute-start = (bf16[192,256]{1,0:T(8,128)(2,1)S(1)}, bf16[192,256]{1,0:T(8,128)(2,1)S(1)}, u32[]{:S(2)}, u32[]{:S(2)}) collective-permute-start(bf16[192,256]{1,0:T(8,128)(2,1)S(1)} %copy.16), channel_id=1, source_target_pairs={{0,8},{8,16},{16,24},{24,32},{32,40},{40,48},{48,56},{56,64},{64,7... | collective-permute-start | bytes 294920 | tf_op jit(solution)/shard_map/while/body/eval_jaxpr/ppermute | solution.py:12
  158.0 17.9 %collective-permute-start = (bf16[192,256]{1,0:T(8,128)(2,1)S(1)}, bf16[192,256]{1,0:T(8,128)(2,1)S(1)}, u32[]{:S(2)}, u32[]{:S(2)}) collective-permute-start(bf16[192,256]{1,0:T(8,128)(2,1)S(1)} %copy.16), channel_id=1, source_target_pairs={{0,8},{8,16},{16,24},{24,32},{32,40},{40,48},{48,56},{56,64},{64,7... | collective-permute-start | bytes 294920 | tf_op jit(solution)/shard_map/while/body/eval_jaxpr/ppermute | solution.py:12
  161.0 14.9 %collective-permute-start.4 = (f32[192,256]{1,0:T(8,128)S(1)}, f32[192,256]{1,0:T(8,128)S(1)}, u32[]{:S(2)}, u32[]{:S(2)}) collective-permute-start(f32[192,256]{1,0:T(8,128)S(1)} %convolution_add_fusion.2), channel_id=1, source_target_pairs={{0,8},{8,16},{16,24},{24,32},{32,40},{40,48},{48,56},{56,64},{64,7... | collective-permute-start | bytes 589832 | tf_op jit(solution)/shard_map/while/body/eval_jaxpr/ppermute | solution.py:12
  175.9 19.1 %collective-permute-start = (bf16[192,256]{1,0:T(8,128)(2,1)S(1)}, bf16[192,256]{1,0:T(8,128)(2,1)S(1)}, u32[]{:S(2)}, u32[]{:S(2)}) collective-permute-start(bf16[192,256]{1,0:T(8,128)(2,1)S(1)} %copy.16), channel_id=1, source_target_pairs={{0,8},{8,16},{16,24},{24,32},{32,40},{40,48},{48,56},{56,64},{64,7... | collective-permute-start | bytes 294920 | tf_op jit(solution)/shard_map/while/body/eval_jaxpr/ppermute | solution.py:12
  178.8 16.1 %collective-permute-start.4 = (f32[192,256]{1,0:T(8,128)S(1)}, f32[192,256]{1,0:T(8,128)S(1)}, u32[]{:S(2)}, u32[]{:S(2)}) collective-permute-start(f32[192,256]{1,0:T(8,128)S(1)} %convolution_add_fusion.2), channel_id=1, source_target_pairs={{0,8},{8,16},{16,24},{24,32},{32,40},{40,48},{48,56},{56,64},{64,7... | collective-permute-start | bytes 589832 | tf_op jit(solution)/shard_map/while/body/eval_jaxpr/ppermute | solution.py:12
  180.2 14.8 %collective-permute-start.5 = (bf16[192,256]{1,0:T(8,128)(2,1)S(1)}, bf16[192,256]{1,0:T(8,128)(2,1)S(1)}, u32[]{:S(2)}, u32[]{:S(2)}) collective-permute-start(bf16[192,256]{1,0:T(8,128)(2,1)S(1)} %fusion.22), channel_id=1, source_target_pairs={{0,8},{8,16},{16,24},{24,32},{32,40},{40,48},{48,56},{56,64},{64,7... | collective-permute-start | bytes 294920 | tf_op jit(solution)/shard_map/while/body/eval_jaxpr/ppermute | solution.py:12
  195.0 18.9 %collective-permute-start = (bf16[192,256]{1,0:T(8,128)(2,1)S(1)}, bf16[192,256]{1,0:T(8,128)(2,1)S(1)}, u32[]{:S(2)}, u32[]{:S(2)}) collective-permute-start(bf16[192,256]{1,0:T(8,128)(2,1)S(1)} %copy.16), channel_id=1, source_target_pairs={{0,8},{8,16},{16,24},{24,32},{32,40},{40,48},{48,56},{56,64},{64,7... | collective-permute-start | bytes 294920 | tf_op jit(solution)/shard_map/while/body/eval_jaxpr/ppermute | solution.py:12
  198.0 15.9 %collective-permute-start.4 = (f32[192,256]{1,0:T(8,128)S(1)}, f32[192,256]{1,0:T(8,128)S(1)}, u32[]{:S(2)}, u32[]{:S(2)}) collective-permute-start(f32[192,256]{1,0:T(8,128)S(1)} %convolution_add_fusion.2), channel_id=1, source_target_pairs={{0,8},{8,16},{16,24},{24,32},{32,40},{40,48},{48,56},{56,64},{64,7... | collective-permute-start | bytes 589832 | tf_op jit(solution)/shard_map/while/body/eval_jaxpr/ppermute | solution.py:12
  199.3 14.5 %collective-permute-start.5 = (bf16[192,256]{1,0:T(8,128)(2,1)S(1)}, bf16[192,256]{1,0:T(8,128)(2,1)S(1)}, u32[]{:S(2)}, u32[]{:S(2)}) collective-permute-start(bf16[192,256]{1,0:T(8,128)(2,1)S(1)} %fusion.22), channel_id=1, source_target_pairs={{0,8},{8,16},{16,24},{24,32},{32,40},{40,48},{48,56},{56,64},{64,7... | collective-permute-start | bytes 294920 | tf_op jit(solution)/shard_map/while/body/eval_jaxpr/ppermute | solution.py:12
  213.9 17.8 %collective-permute-start = (bf16[192,256]{1,0:T(8,128)(2,1)S(1)}, bf16[192,256]{1,0:T(8,128)(2,1)S(1)}, u32[]{:S(2)}, u32[]{:S(2)}) collective-permute-start(bf16[192,256]{1,0:T(8,128)(2,1)S(1)} %copy.16), channel_id=1, source_target_pairs={{0,8},{8,16},{16,24},{24,32},{32,40},{40,48},{48,56},{56,64},{64,7... | collective-permute-start | bytes 294920 | tf_op jit(solution)/shard_map/while/body/eval_jaxpr/ppermute | solution.py:12
  216.8 14.9 %collective-permute-start.4 = (f32[192,256]{1,0:T(8,128)S(1)}, f32[192,256]{1,0:T(8,128)S(1)}, u32[]{:S(2)}, u32[]{:S(2)}) collective-permute-start(f32[192,256]{1,0:T(8,128)S(1)} %convolution_add_fusion.2), channel_id=1, source_target_pairs={{0,8},{8,16},{16,24},{24,32},{32,40},{40,48},{48,56},{56,64},{64,7... | collective-permute-start | bytes 589832 | tf_op jit(solution)/shard_map/while/body/eval_jaxpr/ppermute | solution.py:12
  231.8 17.1 %collective-permute-start = (bf16[192,256]{1,0:T(8,128)(2,1)S(1)}, bf16[192,256]{1,0:T(8,128)(2,1)S(1)}, u32[]{:S(2)}, u32[]{:S(2)}) collective-permute-start(bf16[192,256]{1,0:T(8,128)(2,1)S(1)} %copy.16), channel_id=1, source_target_pairs={{0,8},{8,16},{16,24},{24,32},{32,40},{40,48},{48,56},{56,64},{64,7... | collective-permute-start | bytes 294920 | tf_op jit(solution)/shard_map/while/body/eval_jaxpr/ppermute | solution.py:12
  234.7 14.1 %collective-permute-start.4 = (f32[192,256]{1,0:T(8,128)S(1)}, f32[192,256]{1,0:T(8,128)S(1)}, u32[]{:S(2)}, u32[]{:S(2)}) collective-permute-start(f32[192,256]{1,0:T(8,128)S(1)} %convolution_add_fusion.2), channel_id=1, source_target_pairs={{0,8},{8,16},{16,24},{24,32},{32,40},{40,48},{48,56},{56,64},{64,7... | collective-permute-start | bytes 589832 | tf_op jit(solution)/shard_map/while/body/eval_jaxpr/ppermute | solution.py:12
  248.9 17.0 %collective-permute-start = (bf16[192,256]{1,0:T(8,128)(2,1)S(1)}, bf16[192,256]{1,0:T(8,128)(2,1)S(1)}, u32[]{:S(2)}, u32[]{:S(2)}) collective-permute-start(bf16[192,256]{1,0:T(8,128)(2,1)S(1)} %copy.16), channel_id=1, source_target_pairs={{0,8},{8,16},{16,24},{24,32},{32,40},{40,48},{48,56},{56,64},{64,7... | collective-permute-start | bytes 294920 | tf_op jit(solution)/shard_map/while/body/eval_jaxpr/ppermute | solution.py:12
  251.8 14.0 %collective-permute-start.4 = (f32[192,256]{1,0:T(8,128)S(1)}, f32[192,256]{1,0:T(8,128)S(1)}, u32[]{:S(2)}, u32[]{:S(2)}) collective-permute-start(f32[192,256]{1,0:T(8,128)S(1)} %convolution_add_fusion.2), channel_id=1, source_target_pairs={{0,8},{8,16},{16,24},{24,32},{32,40},{40,48},{48,56},{56,64},{64,7... | collective-permute-start | bytes 589832 | tf_op jit(solution)/shard_map/while/body/eval_jaxpr/ppermute | solution.py:12
  265.9 16.8 %collective-permute-start = (bf16[192,256]{1,0:T(8,128)(2,1)S(1)}, bf16[192,256]{1,0:T(8,128)(2,1)S(1)}, u32[]{:S(2)}, u32[]{:S(2)}) collective-permute-start(bf16[192,256]{1,0:T(8,128)(2,1)S(1)} %copy.16), channel_id=1, source_target_pairs={{0,8},{8,16},{16,24},{24,32},{32,40},{40,48},{48,56},{56,64},{64,7... | collective-permute-start | bytes 294920 | tf_op jit(solution)/shard_map/while/body/eval_jaxpr/ppermute | solution.py:12
  268.9 13.8 %collective-permute-start.4 = (f32[192,256]{1,0:T(8,128)S(1)}, f32[192,256]{1,0:T(8,128)S(1)}, u32[]{:S(2)}, u32[]{:S(2)}) collective-permute-start(f32[192,256]{1,0:T(8,128)S(1)} %convolution_add_fusion.2), channel_id=1, source_target_pairs={{0,8},{8,16},{16,24},{24,32},{32,40},{40,48},{48,56},{56,64},{64,7... | collective-permute-start | bytes 589832 | tf_op jit(solution)/shard_map/while/body/eval_jaxpr/ppermute | solution.py:12
  282.7 16.8 %collective-permute-start = (bf16[192,256]{1,0:T(8,128)(2,1)S(1)}, bf16[192,256]{1,0:T(8,128)(2,1)S(1)}, u32[]{:S(2)}, u32[]{:S(2)}) collective-permute-start(bf16[192,256]{1,0:T(8,128)(2,1)S(1)} %copy.16), channel_id=1, source_target_pairs={{0,8},{8,16},{16,24},{24,32},{32,40},{40,48},{48,56},{56,64},{64,7... | collective-permute-start | bytes 294920 | tf_op jit(solution)/shard_map/while/body/eval_jaxpr/ppermute | solution.py:12
  299.5 16.7 %collective-permute-start = (bf16[192,256]{1,0:T(8,128)(2,1)S(1)}, bf16[192,256]{1,0:T(8,128)(2,1)S(1)}, u32[]{:S(2)}, u32[]{:S(2)}) collective-permute-start(bf16[192,256]{1,0:T(8,128)(2,1)S(1)} %copy.16), channel_id=1, source_target_pairs={{0,8},{8,16},{16,24},{24,32},{32,40},{40,48},{48,56},{56,64},{64,7... | collective-permute-start | bytes 294920 | tf_op jit(solution)/shard_map/while/body/eval_jaxpr/ppermute | solution.py:12
  316.3 17.8 %collective-permute-start = (bf16[192,256]{1,0:T(8,128)(2,1)S(1)}, bf16[192,256]{1,0:T(8,128)(2,1)S(1)}, u32[]{:S(2)}, u32[]{:S(2)}) collective-permute-start(bf16[192,256]{1,0:T(8,128)(2,1)S(1)} %copy.16), channel_id=1, source_target_pairs={{0,8},{8,16},{16,24},{24,32},{32,40},{40,48},{48,56},{56,64},{64,7... | collective-permute-start | bytes 294920 | tf_op jit(solution)/shard_map/while/body/eval_jaxpr/ppermute | solution.py:12
  319.2 14.9 %collective-permute-start.4 = (f32[192,256]{1,0:T(8,128)S(1)}, f32[192,256]{1,0:T(8,128)S(1)}, u32[]{:S(2)}, u32[]{:S(2)}) collective-permute-start(f32[192,256]{1,0:T(8,128)S(1)} %convolution_add_fusion.2), channel_id=1, source_target_pairs={{0,8},{8,16},{16,24},{24,32},{32,40},{40,48},{48,56},{56,64},{64,7... | collective-permute-start | bytes 589832 | tf_op jit(solution)/shard_map/while/body/eval_jaxpr/ppermute | solution.py:12
  334.2 19.1 %collective-permute-start = (bf16[192,256]{1,0:T(8,128)(2,1)S(1)}, bf16[192,256]{1,0:T(8,128)(2,1)S(1)}, u32[]{:S(2)}, u32[]{:S(2)}) collective-permute-start(bf16[192,256]{1,0:T(8,128)(2,1)S(1)} %copy.16), channel_id=1, source_target_pairs={{0,8},{8,16},{16,24},{24,32},{32,40},{40,48},{48,56},{56,64},{64,7... | collective-permute-start | bytes 294920 | tf_op jit(solution)/shard_map/while/body/eval_jaxpr/ppermute | solution.py:12
  337.1 16.1 %collective-permute-start.4 = (f32[192,256]{1,0:T(8,128)S(1)}, f32[192,256]{1,0:T(8,128)S(1)}, u32[]{:S(2)}, u32[]{:S(2)}) collective-permute-start(f32[192,256]{1,0:T(8,128)S(1)} %convolution_add_fusion.2), channel_id=1, source_target_pairs={{0,8},{8,16},{16,24},{24,32},{32,40},{40,48},{48,56},{56,64},{64,7... | collective-permute-start | bytes 589832 | tf_op jit(solution)/shard_map/while/body/eval_jaxpr/ppermute | solution.py:12
  338.5 14.8 %collective-permute-start.5 = (bf16[192,256]{1,0:T(8,128)(2,1)S(1)}, bf16[192,256]{1,0:T(8,128)(2,1)S(1)}, u32[]{:S(2)}, u32[]{:S(2)}) collective-permute-start(bf16[192,256]{1,0:T(8,128)(2,1)S(1)} %fusion.22), channel_id=1, source_target_pairs={{0,8},{8,16},{16,24},{24,32},{32,40},{40,48},{48,56},{56,64},{64,7... | collective-permute-start | bytes 294920 | tf_op jit(solution)/shard_map/while/body/eval_jaxpr/ppermute | solution.py:12
  353.3 18.9 %collective-permute-start = (bf16[192,256]{1,0:T(8,128)(2,1)S(1)}, bf16[192,256]{1,0:T(8,128)(2,1)S(1)}, u32[]{:S(2)}, u32[]{:S(2)}) collective-permute-start(bf16[192,256]{1,0:T(8,128)(2,1)S(1)} %copy.16), channel_id=1, source_target_pairs={{0,8},{8,16},{16,24},{24,32},{32,40},{40,48},{48,56},{56,64},{64,7... | collective-permute-start | bytes 294920 | tf_op jit(solution)/shard_map/while/body/eval_jaxpr/ppermute | solution.py:12
  356.2 15.9 %collective-permute-start.4 = (f32[192,256]{1,0:T(8,128)S(1)}, f32[192,256]{1,0:T(8,128)S(1)}, u32[]{:S(2)}, u32[]{:S(2)}) collective-permute-start(f32[192,256]{1,0:T(8,128)S(1)} %convolution_add_fusion.2), channel_id=1, source_target_pairs={{0,8},{8,16},{16,24},{24,32},{32,40},{40,48},{48,56},{56,64},{64,7... | collective-permute-start | bytes 589832 | tf_op jit(solution)/shard_map/while/body/eval_jaxpr/ppermute | solution.py:12
  357.6 14.5 %collective-permute-start.5 = (bf16[192,256]{1,0:T(8,128)(2,1)S(1)}, bf16[192,256]{1,0:T(8,128)(2,1)S(1)}, u32[]{:S(2)}, u32[]{:S(2)}) collective-permute-start(bf16[192,256]{1,0:T(8,128)(2,1)S(1)} %fusion.22), channel_id=1, source_target_pairs={{0,8},{8,16},{16,24},{24,32},{32,40},{40,48},{48,56},{56,64},{64,7... | collective-permute-start | bytes 294920 | tf_op jit(solution)/shard_map/while/body/eval_jaxpr/ppermute | solution.py:12
  372.2 17.8 %collective-permute-start = (bf16[192,256]{1,0:T(8,128)(2,1)S(1)}, bf16[192,256]{1,0:T(8,128)(2,1)S(1)}, u32[]{:S(2)}, u32[]{:S(2)}) collective-permute-start(bf16[192,256]{1,0:T(8,128)(2,1)S(1)} %copy.16), channel_id=1, source_target_pairs={{0,8},{8,16},{16,24},{24,32},{32,40},{40,48},{48,56},{56,64},{64,7... | collective-permute-start | bytes 294920 | tf_op jit(solution)/shard_map/while/body/eval_jaxpr/ppermute | solution.py:12
  375.1 14.9 %collective-permute-start.4 = (f32[192,256]{1,0:T(8,128)S(1)}, f32[192,256]{1,0:T(8,128)S(1)}, u32[]{:S(2)}, u32[]{:S(2)}) collective-permute-start(f32[192,256]{1,0:T(8,128)S(1)} %convolution_add_fusion.2), channel_id=1, source_target_pairs={{0,8},{8,16},{16,24},{24,32},{32,40},{40,48},{48,56},{56,64},{64,7... | collective-permute-start | bytes 589832 | tf_op jit(solution)/shard_map/while/body/eval_jaxpr/ppermute | solution.py:12
  390.0 17.1 %collective-permute-start = (bf16[192,256]{1,0:T(8,128)(2,1)S(1)}, bf16[192,256]{1,0:T(8,128)(2,1)S(1)}, u32[]{:S(2)}, u32[]{:S(2)}) collective-permute-start(bf16[192,256]{1,0:T(8,128)(2,1)S(1)} %copy.16), channel_id=1, source_target_pairs={{0,8},{8,16},{16,24},{24,32},{32,40},{40,48},{48,56},{56,64},{64,7... | collective-permute-start | bytes 294920 | tf_op jit(solution)/shard_map/while/body/eval_jaxpr/ppermute | solution.py:12
  393.0 14.1 %collective-permute-start.4 = (f32[192,256]{1,0:T(8,128)S(1)}, f32[192,256]{1,0:T(8,128)S(1)}, u32[]{:S(2)}, u32[]{:S(2)}) collective-permute-start(f32[192,256]{1,0:T(8,128)S(1)} %convolution_add_fusion.2), channel_id=1, source_target_pairs={{0,8},{8,16},{16,24},{24,32},{32,40},{40,48},{48,56},{56,64},{64,7... | collective-permute-start | bytes 589832 | tf_op jit(solution)/shard_map/while/body/eval_jaxpr/ppermute | solution.py:12
  407.1 17.0 %collective-permute-start = (bf16[192,256]{1,0:T(8,128)(2,1)S(1)}, bf16[192,256]{1,0:T(8,128)(2,1)S(1)}, u32[]{:S(2)}, u32[]{:S(2)}) collective-permute-start(bf16[192,256]{1,0:T(8,128)(2,1)S(1)} %copy.16), channel_id=1, source_target_pairs={{0,8},{8,16},{16,24},{24,32},{32,40},{40,48},{48,56},{56,64},{64,7... | collective-permute-start | bytes 294920 | tf_op jit(solution)/shard_map/while/body/eval_jaxpr/ppermute | solution.py:12
  410.1 14.0 %collective-permute-start.4 = (f32[192,256]{1,0:T(8,128)S(1)}, f32[192,256]{1,0:T(8,128)S(1)}, u32[]{:S(2)}, u32[]{:S(2)}) collective-permute-start(f32[192,256]{1,0:T(8,128)S(1)} %convolution_add_fusion.2), channel_id=1, source_target_pairs={{0,8},{8,16},{16,24},{24,32},{32,40},{40,48},{48,56},{56,64},{64,7... | collective-permute-start | bytes 589832 | tf_op jit(solution)/shard_map/while/body/eval_jaxpr/ppermute | solution.py:12
  424.2 16.8 %collective-permute-start = (bf16[192,256]{1,0:T(8,128)(2,1)S(1)}, bf16[192,256]{1,0:T(8,128)(2,1)S(1)}, u32[]{:S(2)}, u32[]{:S(2)}) collective-permute-start(bf16[192,256]{1,0:T(8,128)(2,1)S(1)} %copy.16), channel_id=1, source_target_pairs={{0,8},{8,16},{16,24},{24,32},{32,40},{40,48},{48,56},{56,64},{64,7... | collective-permute-start | bytes 294920 | tf_op jit(solution)/shard_map/while/body/eval_jaxpr/ppermute | solution.py:12
  427.1 13.8 %collective-permute-start.4 = (f32[192,256]{1,0:T(8,128)S(1)}, f32[192,256]{1,0:T(8,128)S(1)}, u32[]{:S(2)}, u32[]{:S(2)}) collective-permute-start(f32[192,256]{1,0:T(8,128)S(1)} %convolution_add_fusion.2), channel_id=1, source_target_pairs={{0,8},{8,16},{16,24},{24,32},{32,40},{40,48},{48,56},{56,64},{64,7... | collective-permute-start | bytes 589832 | tf_op jit(solution)/shard_map/while/body/eval_jaxpr/ppermute | solution.py:12
  441.0 16.8 %collective-permute-start = (bf16[192,256]{1,0:T(8,128)(2,1)S(1)}, bf16[192,256]{1,0:T(8,128)(2,1)S(1)}, u32[]{:S(2)}, u32[]{:S(2)}) collective-permute-start(bf16[192,256]{1,0:T(8,128)(2,1)S(1)} %copy.16), channel_id=1, source_target_pairs={{0,8},{8,16},{16,24},{24,32},{32,40},{40,48},{48,56},{56,64},{64,7... | collective-permute-start | bytes 294920 | tf_op jit(solution)/shard_map/while/body/eval_jaxpr/ppermute | solution.py:12
  457.8 16.7 %collective-permute-start = (bf16[192,256]{1,0:T(8,128)(2,1)S(1)}, bf16[192,256]{1,0:T(8,128)(2,1)S(1)}, u32[]{:S(2)}, u32[]{:S(2)}) collective-permute-start(bf16[192,256]{1,0:T(8,128)(2,1)S(1)} %copy.16), channel_id=1, source_target_pairs={{0,8},{8,16},{16,24},{24,32},{32,40},{40,48},{48,56},{56,64},{64,7... | collective-permute-start | bytes 294920 | tf_op jit(solution)/shard_map/while/body/eval_jaxpr/ppermute | solution.py:12
  474.5 17.8 %collective-permute-start = (bf16[192,256]{1,0:T(8,128)(2,1)S(1)}, bf16[192,256]{1,0:T(8,128)(2,1)S(1)}, u32[]{:S(2)}, u32[]{:S(2)}) collective-permute-start(bf16[192,256]{1,0:T(8,128)(2,1)S(1)} %copy.16), channel_id=1, source_target_pairs={{0,8},{8,16},{16,24},{24,32},{32,40},{40,48},{48,56},{56,64},{64,7... | collective-permute-start | bytes 294920 | tf_op jit(solution)/shard_map/while/body/eval_jaxpr/ppermute | solution.py:12
  477.5 14.9 %collective-permute-start.4 = (f32[192,256]{1,0:T(8,128)S(1)}, f32[192,256]{1,0:T(8,128)S(1)}, u32[]{:S(2)}, u32[]{:S(2)}) collective-permute-start(f32[192,256]{1,0:T(8,128)S(1)} %convolution_add_fusion.2), channel_id=1, source_target_pairs={{0,8},{8,16},{16,24},{24,32},{32,40},{40,48},{48,56},{56,64},{64,7... | collective-permute-start | bytes 589832 | tf_op jit(solution)/shard_map/while/body/eval_jaxpr/ppermute | solution.py:12
  492.4 19.1 %collective-permute-start = (bf16[192,256]{1,0:T(8,128)(2,1)S(1)}, bf16[192,256]{1,0:T(8,128)(2,1)S(1)}, u32[]{:S(2)}, u32[]{:S(2)}) collective-permute-start(bf16[192,256]{1,0:T(8,128)(2,1)S(1)} %copy.16), channel_id=1, source_target_pairs={{0,8},{8,16},{16,24},{24,32},{32,40},{40,48},{48,56},{56,64},{64,7... | collective-permute-start | bytes 294920 | tf_op jit(solution)/shard_map/while/body/eval_jaxpr/ppermute | solution.py:12
  495.3 16.1 %collective-permute-start.4 = (f32[192,256]{1,0:T(8,128)S(1)}, f32[192,256]{1,0:T(8,128)S(1)}, u32[]{:S(2)}, u32[]{:S(2)}) collective-permute-start(f32[192,256]{1,0:T(8,128)S(1)} %convolution_add_fusion.2), channel_id=1, source_target_pairs={{0,8},{8,16},{16,24},{24,32},{32,40},{40,48},{48,56},{56,64},{64,7... | collective-permute-start | bytes 589832 | tf_op jit(solution)/shard_map/while/body/eval_jaxpr/ppermute | solution.py:12
  496.7 14.8 %collective-permute-start.5 = (bf16[192,256]{1,0:T(8,128)(2,1)S(1)}, bf16[192,256]{1,0:T(8,128)(2,1)S(1)}, u32[]{:S(2)}, u32[]{:S(2)}) collective-permute-start(bf16[192,256]{1,0:T(8,128)(2,1)S(1)} %fusion.22), channel_id=1, source_target_pairs={{0,8},{8,16},{16,24},{24,32},{32,40},{40,48},{48,56},{56,64},{64,7... | collective-permute-start | bytes 294920 | tf_op jit(solution)/shard_map/while/body/eval_jaxpr/ppermute | solution.py:12
  511.5 18.9 %collective-permute-start = (bf16[192,256]{1,0:T(8,128)(2,1)S(1)}, bf16[192,256]{1,0:T(8,128)(2,1)S(1)}, u32[]{:S(2)}, u32[]{:S(2)}) collective-permute-start(bf16[192,256]{1,0:T(8,128)(2,1)S(1)} %copy.16), channel_id=1, source_target_pairs={{0,8},{8,16},{16,24},{24,32},{32,40},{40,48},{48,56},{56,64},{64,7... | collective-permute-start | bytes 294920 | tf_op jit(solution)/shard_map/while/body/eval_jaxpr/ppermute | solution.py:12
  514.5 15.9 %collective-permute-start.4 = (f32[192,256]{1,0:T(8,128)S(1)}, f32[192,256]{1,0:T(8,128)S(1)}, u32[]{:S(2)}, u32[]{:S(2)}) collective-permute-start(f32[192,256]{1,0:T(8,128)S(1)} %convolution_add_fusion.2), channel_id=1, source_target_pairs={{0,8},{8,16},{16,24},{24,32},{32,40},{40,48},{48,56},{56,64},{64,7... | collective-permute-start | bytes 589832 | tf_op jit(solution)/shard_map/while/body/eval_jaxpr/ppermute | solution.py:12
  515.8 14.5 %collective-permute-start.5 = (bf16[192,256]{1,0:T(8,128)(2,1)S(1)}, bf16[192,256]{1,0:T(8,128)(2,1)S(1)}, u32[]{:S(2)}, u32[]{:S(2)}) collective-permute-start(bf16[192,256]{1,0:T(8,128)(2,1)S(1)} %fusion.22), channel_id=1, source_target_pairs={{0,8},{8,16},{16,24},{24,32},{32,40},{40,48},{48,56},{56,64},{64,7... | collective-permute-start | bytes 294920 | tf_op jit(solution)/shard_map/while/body/eval_jaxpr/ppermute | solution.py:12
  530.4 17.8 %collective-permute-start = (bf16[192,256]{1,0:T(8,128)(2,1)S(1)}, bf16[192,256]{1,0:T(8,128)(2,1)S(1)}, u32[]{:S(2)}, u32[]{:S(2)}) collective-permute-start(bf16[192,256]{1,0:T(8,128)(2,1)S(1)} %copy.16), channel_id=1, source_target_pairs={{0,8},{8,16},{16,24},{24,32},{32,40},{40,48},{48,56},{56,64},{64,7... | collective-permute-start | bytes 294920 | tf_op jit(solution)/shard_map/while/body/eval_jaxpr/ppermute | solution.py:12
  533.3 14.9 %collective-permute-start.4 = (f32[192,256]{1,0:T(8,128)S(1)}, f32[192,256]{1,0:T(8,128)S(1)}, u32[]{:S(2)}, u32[]{:S(2)}) collective-permute-start(f32[192,256]{1,0:T(8,128)S(1)} %convolution_add_fusion.2), channel_id=1, source_target_pairs={{0,8},{8,16},{16,24},{24,32},{32,40},{40,48},{48,56},{56,64},{64,7... | collective-permute-start | bytes 589832 | tf_op jit(solution)/shard_map/while/body/eval_jaxpr/ppermute | solution.py:12
  548.3 17.1 %collective-permute-start = (bf16[192,256]{1,0:T(8,128)(2,1)S(1)}, bf16[192,256]{1,0:T(8,128)(2,1)S(1)}, u32[]{:S(2)}, u32[]{:S(2)}) collective-permute-start(bf16[192,256]{1,0:T(8,128)(2,1)S(1)} %copy.16), channel_id=1, source_target_pairs={{0,8},{8,16},{16,24},{24,32},{32,40},{40,48},{48,56},{56,64},{64,7... | collective-permute-start | bytes 294920 | tf_op jit(solution)/shard_map/while/body/eval_jaxpr/ppermute | solution.py:12
  551.2 14.1 %collective-permute-start.4 = (f32[192,256]{1,0:T(8,128)S(1)}, f32[192,256]{1,0:T(8,128)S(1)}, u32[]{:S(2)}, u32[]{:S(2)}) collective-permute-start(f32[192,256]{1,0:T(8,128)S(1)} %convolution_add_fusion.2), channel_id=1, source_target_pairs={{0,8},{8,16},{16,24},{24,32},{32,40},{40,48},{48,56},{56,64},{64,7... | collective-permute-start | bytes 589832 | tf_op jit(solution)/shard_map/while/body/eval_jaxpr/ppermute | solution.py:12
  565.4 17.0 %collective-permute-start = (bf16[192,256]{1,0:T(8,128)(2,1)S(1)}, bf16[192,256]{1,0:T(8,128)(2,1)S(1)}, u32[]{:S(2)}, u32[]{:S(2)}) collective-permute-start(bf16[192,256]{1,0:T(8,128)(2,1)S(1)} %copy.16), channel_id=1, source_target_pairs={{0,8},{8,16},{16,24},{24,32},{32,40},{40,48},{48,56},{56,64},{64,7... | collective-permute-start | bytes 294920 | tf_op jit(solution)/shard_map/while/body/eval_jaxpr/ppermute | solution.py:12
  568.3 14.0 %collective-permute-start.4 = (f32[192,256]{1,0:T(8,128)S(1)}, f32[192,256]{1,0:T(8,128)S(1)}, u32[]{:S(2)}, u32[]{:S(2)}) collective-permute-start(f32[192,256]{1,0:T(8,128)S(1)} %convolution_add_fusion.2), channel_id=1, source_target_pairs={{0,8},{8,16},{16,24},{24,32},{32,40},{40,48},{48,56},{56,64},{64,7... | collective-permute-start | bytes 589832 | tf_op jit(solution)/shard_map/while/body/eval_jaxpr/ppermute | solution.py:12
  582.4 16.8 %collective-permute-start = (bf16[192,256]{1,0:T(8,128)(2,1)S(1)}, bf16[192,256]{1,0:T(8,128)(2,1)S(1)}, u32[]{:S(2)}, u32[]{:S(2)}) collective-permute-start(bf16[192,256]{1,0:T(8,128)(2,1)S(1)} %copy.16), channel_id=1, source_target_pairs={{0,8},{8,16},{16,24},{24,32},{32,40},{40,48},{48,56},{56,64},{64,7... | collective-permute-start | bytes 294920 | tf_op jit(solution)/shard_map/while/body/eval_jaxpr/ppermute | solution.py:12
  (197 other events, 1457.2 us)
Sparse Core Ops, SparseCore 0:
  689.9 26.0 reduce-scatter.1
where the time goes:
time: 729 us; the launch traced here: 724 us
  waiting for transfers between devices  432 us (59%)
  blocking collectives  112 us (15%)
  matrix products  57.3 us (8%)
  local copies, waits for them, and re-layouts  55.4 us (8%)
  other arithmetic  24 us (3%)
  starting transfers between devices  23.2 us (3%)
  between operations  15.5 us (2%)
    ppermute x224, waiting for transfers between devices, from_behind(): return lax.ppermute(value, axis, pairs)  406 us
    unnamed x2, blocking collectives  97 us
    dot_general x32, matrix products, visit_shard(): lax.dot_general(block_rows, centres, (((1,), (1,)), ((), ())), preferred_...  46.7 us
    gather x32, local copies, waits for them, and re-layouts, visit_shard(): picked = jnp.take(centres, jnp.clip(local_ids, 0, shard_rows - 1), axis=0)  32.1 us
    reduce_scatter x1, waiting for transfers between devices, body(): lax.psum_scatter(partial_grad.astype(jnp.bfloat16), 'group', scatter_dime...  25.6 us
    ppermute x224, starting transfers between devices, from_behind(): return lax.ppermute(value, axis, pairs)  23.2 us
    while x160, local copies, waits for them, and re-layouts  20.5 us
    all_gather x1, blocking collectives, body(): lax.all_gather(student, 'group', axis=0, tiled=True)  14.8 us
  transfers between devices with their start and end apart: 225, of which 85 were waited for; matrix products, arithmetic and copies ran while one was open for 15% of the time, Pallas kernels for 0%

commit v1 on v0

v1 whole, which is shorter than its diff:
```python
import jax
import jax.numpy as jnp
from jax import lax
from jax.experimental import pallas as pl
from jax.experimental.pallas import tpu as pltpu
from jax.sharding import PartitionSpec as P

F32 = jnp.float32
BF16 = jnp.bfloat16
MESH = pl.DeviceIdType.MESH

NX, NY, NZ = 4, 4, 8
NL = NX * NZ
D = 256
QB = 32
OWN = 24
ROWS = OWN * NL
HALF = 512
UNITS = 16
RT = 256
GR = ROWS // 128


def rcopy(src, dst, send, recv, device):
    return pltpu.make_async_remote_copy(
        src_ref=src, dst_ref=dst, send_sem=send, recv_sem=recv, device_id=device, device_id_type=MESH
    )


def joined(tile):
    return jnp.concatenate([tile[:8], tile[8:]], axis=1)


def parted(rows):
    return jnp.concatenate([rows[:, :128], rows[:, 128:]], axis=0)


def kernel(
    exps, tgts, feats, cents, loss_out, grad_out,
    cbuf, ag_a, ag_b, tgb, s32, sbf, tcol, m, l, acc, t, lcol,
    sx, sz, pk_a, pk_b, rx_a, rz_b, q_a, q_b, rz_a, rx_b,
    c_sem, ring_send, unit_recv,
    a1s, a1r, b1s, b1r, t1s, t1r, a2s, a2r, b2s, b2r, t2s, t2r,
    sxs, sxr, szs, szr, ras, rar, rbs, rbr, rcs, rcr, rds, rdr,
):
    loop = lax.axis_index("loop")
    group = lax.axis_index("group")
    x, z = loop // NZ, loop % NZ
    y, core = group // 2, group % 2
    other = 1 - core
    sibling = (loop, y * 2 + other)
    up = (loop, ((y + 1) % NY) * 2 + core)
    down = (loop, ((y + NY - 1) % NY) * 2 + core)

    def at_x(dx):
        return (((x + dx) % NX) * NZ + z, group)

    def at_z(dz):
        return (x * NZ + (z + dz) % NZ, group)

    barrier = pltpu.get_barrier_semaphore()
    partners = [sibling, up, down] + [at_x(d) for d in range(1, NX)] + [at_z(d) for d in range(1, NZ)]
    for partner in partners:
        pl.semaphore_signal(barrier, inc=1, device_id=partner, device_id_type=MESH)

    own = [
        pltpu.make_async_copy(cents.at[pl.ds(h * HALF, HALF)], cbuf.at[h], c_sem.at[h]) for h in range(2)
    ]
    for copy in own:
        copy.start()

    block = lax.broadcasted_iota(jnp.int32, (1, D), 1) // QB
    scale = jnp.zeros((1, D), F32)
    for b in range(D // QB):
        e = exps[b]
        power = jnp.where(e < 0, 0.5, jnp.where(e < 1, 1.0, jnp.where(e < 2, 2.0, 4.0)))
        scale = jnp.where(block == b, power, scale)
    squashed = jnp.tanh(feats[...].astype(F32) / scale)
    student = (scale * squashed).astype(BF16).astype(F32)
    for k in range(2):
        ag_a[loop, k] = parted(student[8 * k : 8 * k + 8]).astype(BF16)
    ag_b[z * NX + x] = parted(student[16:24]).astype(BF16)
    lane = lax.broadcasted_iota(jnp.int32, (1, 128), 1)
    ids = jnp.zeros((1, 128), jnp.int32)
    for i in range(OWN):
        ids = jnp.where(lane == i, tgts[i], ids)
    tgb[loop] = ids

    pl.semaphore_wait(barrier, len(partners))

    sends = []

    def go(copy):
        copy.start()
        sends.append(copy)

    for d in range(1, NZ):
        go(rcopy(ag_a.at[loop], ag_a.at[loop], a1s.at[d - 1], a1r.at[d - 1], at_z(d)))
        go(rcopy(tgb.at[loop], tgb.at[loop], t1s.at[d - 1], t1r.at[d - 1], at_z(d)))
    for d in range(1, NX):
        slot = z * NX + x
        go(rcopy(ag_b.at[slot], ag_b.at[slot], b1s.at[d - 1], b1r.at[d - 1], at_x(d)))

    for copy in own:
        copy.wait()
    go(rcopy(cbuf.at[0], cbuf.at[4], ring_send.at[0], unit_recv.at[4], up))
    go(rcopy(cbuf.at[1], cbuf.at[5], ring_send.at[1], unit_recv.at[5], down))
    go(rcopy(cbuf.at[0], cbuf.at[2], ring_send.at[2], unit_recv.at[2], sibling))
    go(rcopy(cbuf.at[1], cbuf.at[3], ring_send.at[3], unit_recv.at[3], sibling))
    go(rcopy(cbuf.at[1], cbuf.at[6], ring_send.at[4], unit_recv.at[6], up))
    go(rcopy(cbuf.at[0], cbuf.at[7], ring_send.at[5], unit_recv.at[7], down))

    for d in range(1, NZ):
        slot = x * NZ + (z + NZ - d) % NZ
        rcopy(ag_a.at[slot], ag_a.at[slot], a1s.at[d - 1], a1r.at[d - 1], at_z(d)).wait_recv()
        rcopy(tgb.at[slot], tgb.at[slot], t1s.at[d - 1], t1r.at[d - 1], at_z(d)).wait_recv()
    line = pl.ds(x * NZ, NZ)
    for d in range(1, NX):
        go(rcopy(ag_a.at[line], ag_a.at[line], a2s.at[d - 1], a2r.at[d - 1], at_x(d)))
        go(rcopy(tgb.at[line], tgb.at[line], t2s.at[d - 1], t2r.at[d - 1], at_x(d)))
    for d in range(1, NX):
        slot = z * NX + (x + NX - d) % NX
        rcopy(ag_b.at[slot], ag_b.at[slot], b1s.at[d - 1], b1r.at[d - 1], at_x(d)).wait_recv()
    line = pl.ds(z * NX, NX)
    for d in range(1, NZ):
        go(rcopy(ag_b.at[line], ag_b.at[line], b2s.at[d - 1], b2r.at[d - 1], at_z(d)))

    m[...] = jnp.full_like(m, -1e30)
    l[...] = jnp.zeros_like(l)
    acc[...] = jnp.zeros_like(acc)
    t[...] = jnp.zeros_like(t)

    for d in range(1, NX):
        line = pl.ds(((x + NX - d) % NX) * NZ, NZ)
        rcopy(ag_a.at[line], ag_a.at[line], a2s.at[d - 1], a2r.at[d - 1], at_x(d)).wait_recv()
        rcopy(tgb.at[line], tgb.at[line], t2s.at[d - 1], t2r.at[d - 1], at_x(d)).wait_recv()
    for d in range(1, NZ):
        line = pl.ds(((z + NZ - d) % NZ) * NX, NX)
        rcopy(ag_b.at[line], ag_b.at[line], b2s.at[d - 1], b2r.at[d - 1], at_z(d)).wait_recv()

    eye = lax.broadcasted_iota(jnp.int32, (OWN, 128), 0) == lax.broadcasted_iota(jnp.int32, (OWN, 128), 1)

    def unpack(k, _):
        base = pl.multiple_of(k * OWN, 8)
        s32[pl.ds(base, 8), :] = joined(ag_a[k, 0].astype(F32))
        s32[pl.ds(base + 8, 8), :] = joined(ag_a[k, 1].astype(F32))
        s32[pl.ds(base + 16, 8), :] = joined(ag_b[(k % NZ) * NX + k // NZ].astype(F32))
        row = tgb[k].astype(F32)
        column = jnp.sum(jnp.where(eye, row, 0.0), axis=1, keepdims=True)
        tcol[pl.ds(base, OWN), :] = jnp.broadcast_to(column.astype(jnp.int32), (OWN, 128))
        return 0

    lax.fori_loop(0, NL, unpack, 0)
    sbf[...] = s32[...].astype(BF16)

    lanes = lax.broadcasted_iota(jnp.int32, (1, 128), 1)

    def unit(u, base):
        cb = cbuf[u]

        def row_tile(i, _):
            rows = pl.ds(pl.multiple_of(i * RT, RT), RT)
            logits = lax.dot_general(
                sbf[rows, :], cb, (((1,), (1,)), ((), ())), preferred_element_type=F32
            )
            old = m[rows, :]
            new = jnp.maximum(old, jnp.max(logits, axis=1, keepdims=True))
            fade = jnp.exp(old - new)
            m[rows, :] = new
            total = l[rows, :] * fade
            where = tcol[rows, :] - base
            weights, hits = [], []
            for k in range(HALF // 128):
                w = jnp.exp(logits[:, k * 128 : (k + 1) * 128] - new)
                total = total + w
                weights.append(w.astype(BF16))
                hits.append(jnp.where(where == lanes + k * 128, 1.0, 0.0).astype(BF16))
            l[rows, :] = total
            acc[rows, :] = acc[rows, :] * jnp.concatenate([fade, fade], axis=1) + jnp.dot(
                jnp.concatenate(weights, axis=1), cb, preferred_element_type=F32
            )
            t[rows, :] += jnp.dot(jnp.concatenate(hits, axis=1), cb, preferred_element_type=F32)
            return 0

        lax.fori_loop(0, ROWS // RT, row_tile, 0, unroll=True)

    def base_of(dy, c, h):
        return (loop * 2 * NY + ((y + dy) % NY) * 2 + c) * (2 * HALF) + h * HALF

    def arrive(u):
        rcopy(cbuf.at[u], cbuf.at[u], ring_send.at[0], unit_recv.at[u], sibling).wait_recv()

    def run(first, parts):
        def step(j, _):
            base = jnp.int32(0)
            for n, (dy, c, h) in enumerate(parts):
                base = jnp.where(j == n, base_of(dy, c, h), base)
            unit(first + j, base)
            return 0

        lax.fori_loop(0, len(parts), step, 0)

    run(0, [(0, core, 0), (0, core, 1)])
    arrive(2)
    arrive(3)
    run(2, [(0, other, 0), (0, other, 1)])
    arrive(4)
    go(rcopy(cbuf.at[4], cbuf.at[12], ring_send.at[6], unit_recv.at[12], up))
    go(rcopy(cbuf.at[4], cbuf.at[8], ring_send.at[8], unit_recv.at[8], sibling))
    arrive(5)
    go(rcopy(cbuf.at[5], cbuf.at[13], ring_send.at[7], unit_recv.at[13], down))
    go(rcopy(cbuf.at[5], cbuf.at[9], ring_send.at[9], unit_recv.at[9], sibling))
    run(4, [(3, core, 0), (1, core, 1)])
    arrive(6)
    go(rcopy(cbuf.at[6], cbuf.at[10], ring_send.at[10], unit_recv.at[10], sibling))
    arrive(7)
    go(rcopy(cbuf.at[7], cbuf.at[11], ring_send.at[11], unit_recv.at[11], sibling))
    run(6, [(3, core, 1), (1, core, 0)])
    for u in range(8, 12):
        arrive(u)
    run(8, [(3, other, 0), (1, other, 1), (3, other, 1), (1, other, 0)])
    arrive(12)
    go(rcopy(cbuf.at[12], cbuf.at[14], ring_send.at[12], unit_recv.at[14], sibling))
    arrive(13)
    go(rcopy(cbuf.at[13], cbuf.at[15], ring_send.at[13], unit_recv.at[15], sibling))
    run(12, [(2, core, 0), (2, core, 1)])
    arrive(14)
    arrive(15)
    run(14, [(2, other, 0), (2, other, 1)])

    eye128 = lax.broadcasted_iota(jnp.int32, (128, 128), 0) == lax.broadcasted_iota(jnp.int32, (128, 128), 1)

    def as_row(column):
        return jnp.sum(jnp.where(eye128, column, 0.0), axis=0, keepdims=True)

    sx[0] = jnp.zeros((16, 128), F32)
    for g in range(GR):
        rows = pl.ds(g * 128, 128)
        lse = m[rows, :] + jnp.log(jnp.sum(l[rows, :], axis=1, keepdims=True))
        hit = jnp.sum(s32[rows, :] * t[rows, :], axis=1, keepdims=True)
        sx[0, g : g + 1, :] = as_row(lse)
        sx[0, 8 + g : 9 + g, :] = as_row(hit)

    def combine(ref, count):
        parts = [ref[k] for k in range(count)]
        top = parts[0]
        for part in parts[1:]:
            top = jnp.maximum(top, part)
        total = jnp.zeros_like(top)
        plain = jnp.zeros_like(top)
        for part in parts:
            total = total + jnp.exp(part - top)
            plain = plain + part
        first = lax.broadcasted_iota(jnp.int32, (16, 128), 0) < 8
        return jnp.where(first, top + jnp.log(total), plain)

    for d in range(1, NX):
        go(rcopy(sx.at[0], sx.at[d], sxs.at[d - 1], sxr.at[d - 1], at_x(d)))
    for d in range(1, NX):
        rcopy(sx.at[d], sx.at[d], sxs.at[d - 1], sxr.at[d - 1], at_x(d)).wait_recv()
    sz[0] = combine(sx, NX)
    for d in range(1, NZ):
        go(rcopy(sz.at[0], sz.at[d], szs.at[d - 1], szr.at[d - 1], at_z(d)))
    for d in range(1, NZ):
        rcopy(sz.at[d], sz.at[d], szs.at[d - 1], szr.at[d - 1], at_z(d)).wait_recv()
    stats = combine(sz, NZ)
    for g in range(GR):
        lcol[pl.ds(g * 128, 128), :] = jnp.broadcast_to(
            jnp.sum(jnp.where(eye128, stats[g : g + 1, :], 0.0), axis=1, keepdims=True), (128, 128)
        )

    def pack(k, _):
        base = pl.multiple_of(k * OWN, 8)
        rows = pl.ds(base, OWN)
        share = jnp.exp(m[rows, :] - lcol[rows, :])
        part = acc[rows, :] * jnp.concatenate([share, share], axis=1) - t[rows, :]
        pk_a[k, 0] = parted(part[0:8]).astype(BF16)
        pk_a[k, 1] = parted(part[8:16]).astype(BF16)
        pk_b[(k % NZ) * NX + k // NZ] = parted(part[16:24]).astype(BF16)
        return 0

    lax.fori_loop(0, NL, pack, 0)
    for d in range(1, NX):
        line = pl.ds(((x + d) % NX) * NZ, NZ)
        go(rcopy(pk_a.at[line], rx_a.at[d - 1], ras.at[d - 1], rar.at[d - 1], at_x(d)))
    for d in range(1, NZ):
        line = pl.ds(((z + d) % NZ) * NX, NX)
        go(rcopy(pk_b.at[line], rz_b.at[d - 1], rbs.at[d - 1], rbr.at[d - 1], at_z(d)))
    for d in range(1, NX):
        rcopy(rx_a.at[d - 1], rx_a.at[d - 1], ras.at[d - 1], rar.at[d - 1], at_x(d)).wait_recv()
    total = pk_a[pl.ds(x * NZ, NZ)].astype(F32)
    for d in range(1, NX):
        total = total + rx_a[d - 1].astype(F32)
    q_a[...] = total.astype(BF16)
    for d in range(1, NZ):
        go(rcopy(q_a.at[(z + d) % NZ], rz_a.at[d - 1], rcs.at[d - 1], rcr.at[d - 1], at_z(d)))
    for d in range(1, NZ):
        rcopy(rz_b.at[d - 1], rz_b.at[d - 1], rbs.at[d - 1], rbr.at[d - 1], at_z(d)).wait_recv()
    total = pk_b[pl.ds(z * NX, NX)].astype(F32)
    for d in range(1, NZ):
        total = total + rz_b[d - 1].astype(F32)
    q_b[...] = total.astype(BF16)
    for d in range(1, NX):
        go(rcopy(q_b.at[(x + d) % NX], rx_b.at[d - 1], rds.at[d - 1], rdr.at[d - 1], at_x(d)))

    wanted = loop * OWN + lax.broadcasted_iota(jnp.int32, (OWN, 128), 0)
    place = lax.broadcasted_iota(jnp.int32, (OWN, 128), 1)
    column = jnp.zeros((OWN, 1), F32)
    for g in range(GR):
        row = stats[g : g + 1, :] - stats[8 + g : 9 + g, :]
        column = column + jnp.sum(jnp.where(place + g * 128 == wanted, row, 0.0), axis=1, keepdims=True)
    loss_out[...] = jnp.sum(jnp.where(eye, column, 0.0), axis=0, keepdims=True)

    for d in range(1, NZ):
        rcopy(rz_a.at[d - 1], rz_a.at[d - 1], rcs.at[d - 1], rcr.at[d - 1], at_z(d)).wait_recv()
    part_a = q_a[z].astype(F32)
    for d in range(1, NZ):
        part_a = part_a + rz_a[d - 1].astype(F32)
    for d in range(1, NX):
        rcopy(rx_b.at[d - 1], rx_b.at[d - 1], rds.at[d - 1], rdr.at[d - 1], at_x(d)).wait_recv()
    part_b = q_b[x].astype(F32)
    for d in range(1, NX):
        part_b = part_b + rx_b[d - 1].astype(F32)
    grad = jnp.concatenate([joined(part_a[0]), joined(part_a[1]), joined(part_b)], axis=0)
    squashed = jnp.tanh(feats[...].astype(F32) / scale)
    grad_out[...] = grad * (1.0 - squashed * squashed)

    for copy in sends:
        copy.wait_send()


def body(features, scale_exponents, targets, centres):
    def dma(*shape):
        return pltpu.SemaphoreType.DMA(shape)

    vx, vz = [dma(NX - 1)] * 2, [dma(NZ - 1)] * 2
    loss, grad = pl.pallas_call(
        kernel,
        out_shape=(jax.ShapeDtypeStruct((1, 128), F32), jax.ShapeDtypeStruct((OWN, D), F32)),
        in_specs=[
            pl.BlockSpec(memory_space=pltpu.SMEM),
            pl.BlockSpec(memory_space=pltpu.SMEM),
            pl.BlockSpec(memory_space=pltpu.VMEM),
            pl.BlockSpec(memory_space=pl.ANY),
        ],
        out_specs=(pl.BlockSpec(memory_space=pltpu.VMEM), pl.BlockSpec(memory_space=pltpu.VMEM)),
        scratch_shapes=[
            pltpu.VMEM((UNITS, HALF, D), BF16),
            pltpu.VMEM((NL, 2, 16, 128), BF16),
            pltpu.VMEM((NL, 16, 128), BF16),
            pltpu.VMEM((NL, 1, 128), jnp.int32),
            pltpu.VMEM((ROWS, D), F32),
            pltpu.VMEM((ROWS, D), BF16),
            pltpu.VMEM((ROWS, 128), jnp.int32),
            pltpu.VMEM((ROWS, 128), F32),
            pltpu.VMEM((ROWS, 128), F32),
            pltpu.VMEM((ROWS, D), F32),
            pltpu.VMEM((ROWS, D), F32),
            pltpu.VMEM((ROWS, 128), F32),
            pltpu.VMEM((NX, 16, 128), F32),
            pltpu.VMEM((NZ, 16, 128), F32),
            pltpu.VMEM((NL, 2, 16, 128), BF16),
            pltpu.VMEM((NL, 16, 128), BF16),
            pltpu.VMEM((NX - 1, NZ, 2, 16, 128), BF16),
            pltpu.VMEM((NZ - 1, NX, 16, 128), BF16),
            pltpu.VMEM((NZ, 2, 16, 128), BF16),
            pltpu.VMEM((NX, 16, 128), BF16),
            pltpu.VMEM((NZ - 1, 2, 16, 128), BF16),
            pltpu.VMEM((NX - 1, 16, 128), BF16),
            dma(2),
            dma(14),
            dma(UNITS),
            *vz, *vx, *vz, *vx, *vz, *vx,
            *vx, *vz, *vx, *vz, *vz, *vx,
        ],
        compiler_params=pltpu.CompilerParams(
            collective_id=0, has_side_effects=True, vmem_limit_bytes=40 * 1024 * 1024
        ),
    )(scale_exponents, targets, features, centres)
    return loss[0, :OWN], grad


def solution(mesh):
    placed = (P(("loop", "group"), None), P(), P(("loop", "group")), P(("loop", "group"), None))
    return jax.shard_map(
        body,
        mesh=mesh,
        in_specs=placed,
        out_specs=(P(("loop", "group")), P(("loop", "group"), None)),
        check_vma=False,
    )
```

time: 729 us -> 68.7 us (0.09)
  the two profiles are of different devices: /device:TPU:1 before, /device:TPU:8 now
where the time goes in v1:
time: 68.7 us; the launch traced here: 68.5 us
  Pallas kernels  63.7 us (93%)
  local copies, waits for them, and re-layouts  4.17 us (6%)
    pallas_call x1, Pallas kernels, body(): pl.pallas_call(kernel, out_shape=(jax.ShapeDtypeStruct((1, 128), F32), ja...  63.7 us
    unnamed x9, local copies, waits for them, and re-layouts  3.66 us

profile of v1, /device:TPU:8, one launch (start us, length us, event | category | flops | bytes accessed | tf_op | source)
XLA Modules:
  0.0 68.5 jit_solution(17048029320973632597)
XLA Ops:
  0.6 0.0 copy-start
  0.6 1.0 %copy-done = bf16[1024,256]{1,0:T(8,128)(2,1)S(1)} copy-done((bf16[1024,256]{1,0:T(8,128)(2,1)S(1)}, bf16[1024,256]{1,0:T(8,128)(2,1)}, u32[]{:S(2)}) %copy-start) | copy-done | bytes 524312
  1.7 0.0 copy-start.1
  1.7 0.7 %copy-done.1 = bf16[24,256]{1,0:T(8,128)(2,1)S(1)} copy-done((bf16[24,256]{1,0:T(8,128)(2,1)S(1)}, bf16[24,256]{1,0:T(8,128)(2,1)}, u32[]{:S(2)}) %copy-start.1) | copy-done | bytes 12312
  2.4 0.0 copy-start.2
  2.4 0.7 copy-done.2
  3.0 0.0 copy-start.3
  3.0 0.7 copy-done.3
  3.7 63.7 %shard_map.59 = (f32[1,128]{1,0:T(1,128)S(1)}, f32[24,256]{1,0:T(8,128)S(1)}) custom-call(s32[8]{0:T(128)S(1)} %copy-done.2, s32[24]{0:T(128)S(1)} %copy-done.3, bf16[24,256]{1,0:T(8,128)(2,1)S(1)} %copy-done.1, bf16[1024,256]{1,0:T(8,128)(2,1)S(1)} %copy-done), custom_call_target="tpu_custom_call" | custom-call | tf_op jit(solution)/shard_map/pallas_call | solution.py:337
  67.4 0.5 slice_bitcast_fusion
  67.9 0.6 copy.7
Async XLA Ops:
  0.6 1.0 %copy-start = (bf16[1024,256]{1,0:T(8,128)(2,1)S(1)}, bf16[1024,256]{1,0:T(8,128)(2,1)}, u32[]{:S(2)}) copy-start(bf16[1024,256]{1,0:T(8,128)(2,1)} %cents.1) | copy-start | bytes 1572868
  1.7 0.7 %copy-start.1 = (bf16[24,256]{1,0:T(8,128)(2,1)S(1)}, bf16[24,256]{1,0:T(8,128)(2,1)}, u32[]{:S(2)}) copy-start(bf16[24,256]{1,0:T(8,128)(2,1)} %feats.1) | copy-start | bytes 36868
  2.4 0.7 copy-start.2
  3.0 0.7 copy-start.3

commit v2 on v1

v2 whole, which is shorter than its diff:
```python
import jax
import jax.numpy as jnp
from jax import lax
from jax.experimental import pallas as pl
from jax.experimental.pallas import tpu as pltpu
from jax.sharding import PartitionSpec as P

F32 = jnp.float32
BF16 = jnp.bfloat16
MESH = pl.DeviceIdType.MESH

NX, NY, NZ = 4, 4, 8
NL = NX * NZ
D = 256
QB = 32
OWN = 24
ROWS = OWN * NL
HALF = 512
UNITS = 16
RT = 768
RA = 16 * NL


def rcopy(src, dst, send, recv, device):
    return pltpu.make_async_remote_copy(
        src_ref=src, dst_ref=dst, send_sem=send, recv_sem=recv, device_id=device, device_id_type=MESH
    )


def joined(tiles):
    count = tiles.shape[0]
    low = tiles[:, :8].reshape(count * 8, 128)
    high = tiles[:, 8:].reshape(count * 8, 128)
    return jnp.concatenate([low, high], axis=1)


def parted(rows):
    count = rows.shape[0] // 8
    low = rows[:, :128].reshape(count, 8, 128)
    high = rows[:, 128:].reshape(count, 8, 128)
    return jnp.concatenate([low, high], axis=1)


def shares(parts):
    top = parts[0]
    for part in parts[1:]:
        top = jnp.maximum(top, part)
    powers = [jnp.exp(part - top) for part in parts]
    total = powers[0]
    for power in powers[1:]:
        total = total + power
    return top + jnp.log(total), [power / total for power in powers]


def twice(column):
    wide = jnp.broadcast_to(column, (8, 128))
    return jnp.concatenate([wide, wide], axis=0)


def kernel(
    exps_hbm, tgts_hbm, feats_hbm, cents, loss_out, grad_out,
    exps, tgts, feats, cbuf, ag_a, ag_b, tgb, sbf, tcol, m, l, acc, t,
    pk_a, pk_b, ht_a, ht_b, rht_a, rht_b, la, lb, rx_a, rz_b, rla, rlb, q_a, q_b, qla, qlb, rz_a, rx_b, flA, flB,
    in_sem, c_sem, ring_send, unit_recv,
    a1s, a1r, b1s, b1r, t1s, t1r, a2s, a2r, b2s, b2r, t2s, t2r,
    ras, rar, rbs, rbr, rcs, rcr, rds, rdr,
    has, har, hbs, hbr, las, lar, lbs, lbr, lcs, lcr, lds, ldr,
):
    loop = lax.axis_index("loop")
    group = lax.axis_index("group")
    x, z = loop // NZ, loop % NZ
    y, core = group // 2, group % 2
    other = 1 - core
    sibling = (loop, y * 2 + other)
    up = (loop, ((y + 1) % NY) * 2 + core)
    down = (loop, ((y + NY - 1) % NY) * 2 + core)

    def at_x(dx):
        return (((x + dx) % NX) * NZ + z, group)

    def at_z(dz):
        return (x * NZ + (z + dz) % NZ, group)

    barrier = pltpu.get_barrier_semaphore()
    partners = [at_z(d) for d in range(1, NZ)] + [at_x(d) for d in range(1, NX)] + [sibling, up, down]
    for partner in partners:
        pl.semaphore_signal(barrier, inc=1, device_id=partner, device_id_type=MESH)

    small = [
        pltpu.make_async_copy(exps_hbm, exps, in_sem.at[0]),
        pltpu.make_async_copy(tgts_hbm, tgts, in_sem.at[1]),
        pltpu.make_async_copy(feats_hbm, feats, in_sem.at[2]),
    ]
    own = [
        pltpu.make_async_copy(cents.at[pl.ds(h * HALF, HALF)], cbuf.at[h], c_sem.at[h]) for h in range(2)
    ]
    for copy in small + own:
        copy.start()
    for copy in small:
        copy.wait()

    block = lax.broadcasted_iota(jnp.int32, (1, D), 1) // QB
    scale = jnp.zeros((1, D), F32)
    for b in range(D // QB):
        e = exps[b]
        power = jnp.where(e < 0, 0.5, jnp.where(e < 1, 1.0, jnp.where(e < 2, 2.0, 4.0)))
        scale = jnp.where(block == b, power, scale)
    squashed = jnp.tanh(feats[...].astype(F32) / scale)
    student = (scale * squashed).astype(BF16).astype(F32)
    tiles = parted(student).astype(BF16)
    ag_a[loop] = tiles[0:2]
    ag_b[z * NX + x] = tiles[2]
    lane = lax.broadcasted_iota(jnp.int32, (1, 128), 1)
    ids = jnp.zeros((1, 128), jnp.int32)
    for i in range(OWN):
        ids = jnp.where(lane == i, tgts[i], ids)
    tgb[loop] = ids

    pl.semaphore_wait(barrier, len(partners))

    sends = []

    def go(copy):
        copy.start()
        sends.append(copy)

    for d in range(1, NZ):
        go(rcopy(ag_a.at[loop], ag_a.at[loop], a1s.at[d - 1], a1r.at[d - 1], at_z(d)))
    for d in range(1, NX):
        slot = z * NX + x
        go(rcopy(ag_b.at[slot], ag_b.at[slot], b1s.at[d - 1], b1r.at[d - 1], at_x(d)))

    for copy in own:
        copy.wait()
    go(rcopy(cbuf.at[0], cbuf.at[4], ring_send.at[0], unit_recv.at[4], up))
    go(rcopy(cbuf.at[1], cbuf.at[5], ring_send.at[1], unit_recv.at[5], down))
    go(rcopy(cbuf.at[0], cbuf.at[2], ring_send.at[2], unit_recv.at[2], sibling))
    go(rcopy(cbuf.at[1], cbuf.at[3], ring_send.at[3], unit_recv.at[3], sibling))
    go(rcopy(cbuf.at[1], cbuf.at[6], ring_send.at[4], unit_recv.at[6], up))
    go(rcopy(cbuf.at[0], cbuf.at[7], ring_send.at[5], unit_recv.at[7], down))
    for d in range(1, NZ):
        go(rcopy(tgb.at[loop], tgb.at[loop], t1s.at[d - 1], t1r.at[d - 1], at_z(d)))

    for d in range(1, NZ):
        slot = x * NZ + (z + NZ - d) % NZ
        rcopy(ag_a.at[slot], ag_a.at[slot], a1s.at[d - 1], a1r.at[d - 1], at_z(d)).wait_recv()
    line = pl.ds(x * NZ, NZ)
    for d in range(1, NX):
        go(rcopy(ag_a.at[line], ag_a.at[line], a2s.at[d - 1], a2r.at[d - 1], at_x(d)))
    for d in range(1, NX):
        slot = z * NX + (x + NX - d) % NX
        rcopy(ag_b.at[slot], ag_b.at[slot], b1s.at[d - 1], b1r.at[d - 1], at_x(d)).wait_recv()
    line = pl.ds(z * NX, NX)
    for d in range(1, NZ):
        go(rcopy(ag_b.at[line], ag_b.at[line], b2s.at[d - 1], b2r.at[d - 1], at_z(d)))
    for d in range(1, NZ):
        slot = x * NZ + (z + NZ - d) % NZ
        rcopy(tgb.at[slot], tgb.at[slot], t1s.at[d - 1], t1r.at[d - 1], at_z(d)).wait_recv()
    line = pl.ds(x * NZ, NZ)
    for d in range(1, NX):
        go(rcopy(tgb.at[line], tgb.at[line], t2s.at[d - 1], t2r.at[d - 1], at_x(d)))

    m[...] = jnp.full_like(m, -1e30)
    l[...] = jnp.zeros_like(l)
    acc[...] = jnp.zeros_like(acc)
    t[...] = jnp.zeros_like(t)

    for d in range(1, NX):
        line = pl.ds(((x + NX - d) % NX) * NZ, NZ)
        rcopy(ag_a.at[line], ag_a.at[line], a2s.at[d - 1], a2r.at[d - 1], at_x(d)).wait_recv()
    sbf[0:RA, :] = joined(ag_a[...].astype(F32).reshape(2 * NL, 16, 128)).astype(BF16)
    for d in range(1, NX):
        line = pl.ds(((x + NX - d) % NX) * NZ, NZ)
        rcopy(tgb.at[line], tgb.at[line], t2s.at[d - 1], t2r.at[d - 1], at_x(d)).wait_recv()
    eye = lax.broadcasted_iota(jnp.int32, (OWN, 128), 0) == lax.broadcasted_iota(jnp.int32, (OWN, 128), 1)
    for k in range(NL):
        row = tgb[k].astype(F32)
        column = jnp.sum(jnp.where(eye, row, 0.0), axis=1, keepdims=True).astype(jnp.int32)
        slot = (k % NZ) * NX + k // NZ
        tcol[16 * k : 16 * k + 16, :] = jnp.broadcast_to(column[:16], (16, 128))
        tcol[RA + 8 * slot : RA + 8 * slot + 8, :] = jnp.broadcast_to(column[16:], (8, 128))
    for d in range(1, NZ):
        line = pl.ds(((z + NZ - d) % NZ) * NX, NX)
        rcopy(ag_b.at[line], ag_b.at[line], b2s.at[d - 1], b2r.at[d - 1], at_z(d)).wait_recv()
    sbf[RA:ROWS, :] = joined(ag_b[...].astype(F32)).astype(BF16)

    lanes = lax.broadcasted_iota(jnp.int32, (1, 128), 1)

    def chunk(u, bases, soft=True, pick=True):
        def row_tile(i, _):
            rows = pl.ds(pl.multiple_of(i * RT, RT), RT)
            cb = jnp.concatenate([cbuf[u + n] for n in range(len(bases))], axis=0)
            if soft:
                logits = lax.dot_general(
                    sbf[rows, :], cb, (((1,), (1,)), ((), ())), preferred_element_type=F32
                )
                old = m[rows, :]
                new = jnp.maximum(old, jnp.max(logits, axis=1, keepdims=True))
                fade = jnp.exp(old - new)
                m[rows, :] = new
                total = l[rows, :] * fade
                weights = []
                for k in range(len(bases) * HALF // 128):
                    w = jnp.exp(logits[:, k * 128 : (k + 1) * 128] - new)
                    total = total + w
                    weights.append(w.astype(BF16))
                l[rows, :] = total
                acc[rows, :] = acc[rows, :] * jnp.concatenate([fade, fade], axis=1) + jnp.dot(
                    jnp.concatenate(weights, axis=1), cb, preferred_element_type=F32
                )
            if pick:
                hits = []
                for base in bases:
                    where = tcol[rows, :] - base
                    for k in range(HALF // 128):
                        hits.append(jnp.where(where == lanes + k * 128, 1.0, 0.0).astype(BF16))
                t[rows, :] += jnp.dot(jnp.concatenate(hits, axis=1), cb, preferred_element_type=F32)
            return 0

        lax.fori_loop(0, ROWS // RT, row_tile, 0, unroll=True)

    def bases_of(*parts):
        return [
            (loop * 2 * NY + ((y + dy) % NY) * 2 + c) * (2 * HALF) + h * HALF for dy, c, h in parts
        ]

    def arrive(*units):
        for u in units:
            rcopy(cbuf.at[u], cbuf.at[u], ring_send.at[0], unit_recv.at[u], sibling).wait_recv()

    arrive(4)
    go(rcopy(cbuf.at[4], cbuf.at[12], ring_send.at[6], unit_recv.at[12], up))
    go(rcopy(cbuf.at[4], cbuf.at[8], ring_send.at[8], unit_recv.at[8], sibling))
    arrive(5)
    go(rcopy(cbuf.at[5], cbuf.at[13], ring_send.at[7], unit_recv.at[13], down))
    go(rcopy(cbuf.at[5], cbuf.at[9], ring_send.at[9], unit_recv.at[9], sibling))
    arrive(2, 3)
    chunk(0, bases_of((0, core, 0), (0, core, 1), (0, other, 0), (0, other, 1)))
    arrive(6)
    go(rcopy(cbuf.at[6], cbuf.at[10], ring_send.at[10], unit_recv.at[10], sibling))
    arrive(7)
    go(rcopy(cbuf.at[7], cbuf.at[11], ring_send.at[11], unit_recv.at[11], sibling))
    chunk(4, bases_of((3, core, 0), (1, core, 1), (3, core, 1), (1, core, 0)))
    arrive(8, 9, 10, 11)
    chunk(8, bases_of((3, other, 0), (1, other, 1), (3, other, 1), (1, other, 0)))
    last = bases_of((2, core, 0), (2, core, 1), (2, other, 0), (2, other, 1))
    arrive(12)
    go(rcopy(cbuf.at[12], cbuf.at[14], ring_send.at[12], unit_recv.at[14], sibling))
    arrive(13)
    go(rcopy(cbuf.at[13], cbuf.at[15], ring_send.at[13], unit_recv.at[15], sibling))
    chunk(12, last[:2], pick=False)
    arrive(14, 15)
    chunk(12, last, soft=False)
    for k in range(0, ROWS // 8, 2 * NZ):
        hit = parted(t[8 * k : 8 * k + 16 * NZ, :]).astype(BF16)
        if k < RA // 8:
            ht_a[k // 2 : k // 2 + NZ] = hit.reshape(NZ, 2, 16, 128)
        else:
            ht_b[k - RA // 8 : k - RA // 8 + 2 * NZ] = hit
    for d in range(1, NX):
        to = (x + d) % NX
        go(rcopy(ht_a.at[pl.ds(to * NZ, NZ)], rht_a.at[d - 1], has.at[d - 1], har.at[d - 1], at_x(d)))
    for d in range(1, NZ):
        to = (z + d) % NZ
        go(rcopy(ht_b.at[pl.ds(to * NX, NX)], rht_b.at[d - 1], hbs.at[d - 1], hbr.at[d - 1], at_z(d)))
    chunk(14, last[2:], pick=False)

    block8 = lax.broadcasted_iota(jnp.int32, (8, 128), 1) // 8

    def closed(rows):
        total = jnp.sum(l[rows, :], axis=1, keepdims=True)
        l[rows, :] = m[rows, :] + jnp.log(total)
        return parted(acc[rows, :] * (1.0 / total)).astype(BF16)

    def lanes_of(first, count):
        out = jnp.zeros((8, 128), F32)
        for j in range(count):
            out = jnp.where(block8 == j, l[first + 8 * j : first + 8 * j + 8, :], out)
        return out

    for k in range(NX):
        pk_a[k * NZ : (k + 1) * NZ] = closed(pl.ds(k * 128, 128)).reshape(NZ, 2, 16, 128)
        la[k] = lanes_of(k * 128, 2 * NZ)
    for d in range(1, NX):
        to = (x + d) % NX
        go(rcopy(pk_a.at[pl.ds(to * NZ, NZ)], rx_a.at[d - 1], ras.at[d - 1], rar.at[d - 1], at_x(d)))
        go(rcopy(la.at[to], rla.at[d - 1], las.at[d - 1], lar.at[d - 1], at_x(d)))
    for k in range(0, NZ, 4):
        pk_b[k * NX : (k + 4) * NX] = closed(pl.ds(RA + k * 32, 128))
    for k in range(NZ):
        lb[k] = lanes_of(RA + k * 32, NX)
    for d in range(1, NZ):
        to = (z + d) % NZ
        go(rcopy(pk_b.at[pl.ds(to * NX, NX)], rz_b.at[d - 1], rbs.at[d - 1], rbr.at[d - 1], at_z(d)))
        go(rcopy(lb.at[to], rlb.at[d - 1], lbs.at[d - 1], lbr.at[d - 1], at_z(d)))
    for copy in sends:
        copy.wait_send()
    sends.clear()

    for d in range(1, NX):
        rcopy(rla.at[d - 1], rla.at[d - 1], las.at[d - 1], lar.at[d - 1], at_x(d)).wait_recv()
    for d in range(1, NX):
        rcopy(rht_a.at[d - 1], rht_a.at[d - 1], has.at[d - 1], har.at[d - 1], at_x(d)).wait_recv()
    hit = ht_a[pl.ds(x * NZ, NZ)]
    for d in range(1, NX):
        hit = hit + rht_a[d - 1]
    q_a[:, 1] = hit
    lse, parts = shares([la[x]] + [rla[d - 1] for d in range(1, NX)])
    qla[...] = lse
    for d in range(1, NX):
        rcopy(rx_a.at[d - 1], rx_a.at[d - 1], ras.at[d - 1], rar.at[d - 1], at_x(d)).wait_recv()
    for k in range(NZ):
        got = [pk_a[x * NZ + k]] + [rx_a[d - 1, k] for d in range(1, NX)]
        for j in range(2):
            at = 8 * (2 * k + j)
            mean = jnp.zeros((16, 128), F32)
            for part, tile in zip(parts, got):
                mean = mean + twice(part[:, at : at + 1]) * tile[j].astype(F32)
            q_a[k, 0, j] = mean.astype(BF16)
    for d in range(1, NZ):
        go(rcopy(q_a.at[(z + d) % NZ], rz_a.at[d - 1], rcs.at[d - 1], rcr.at[d - 1], at_z(d)))
        go(rcopy(qla, flA.at[d - 1], lcs.at[d - 1], lcr.at[d - 1], at_z(d)))

    for d in range(1, NZ):
        rcopy(rlb.at[d - 1], rlb.at[d - 1], lbs.at[d - 1], lbr.at[d - 1], at_z(d)).wait_recv()
    for d in range(1, NZ):
        rcopy(rht_b.at[d - 1], rht_b.at[d - 1], hbs.at[d - 1], hbr.at[d - 1], at_z(d)).wait_recv()
    hit = ht_b[pl.ds(z * NX, NX)]
    for d in range(1, NZ):
        hit = hit + rht_b[d - 1]
    q_b[:, 1] = hit
    lse, parts = shares([lb[z]] + [rlb[d - 1] for d in range(1, NZ)])
    qlb[...] = lse
    for d in range(1, NZ):
        rcopy(rz_b.at[d - 1], rz_b.at[d - 1], rbs.at[d - 1], rbr.at[d - 1], at_z(d)).wait_recv()
    for k in range(NX):
        got = [pk_b[z * NX + k]] + [rz_b[d - 1, k] for d in range(1, NZ)]
        mean = jnp.zeros((16, 128), F32)
        for part, tile in zip(parts, got):
            mean = mean + twice(part[:, 8 * k : 8 * k + 1]) * tile.astype(F32)
        q_b[k, 0] = mean.astype(BF16)
    for d in range(1, NX):
        go(rcopy(q_b.at[(x + d) % NX], rx_b.at[d - 1], rds.at[d - 1], rdr.at[d - 1], at_x(d)))
        go(rcopy(qlb, flB.at[d - 1], lds.at[d - 1], ldr.at[d - 1], at_x(d)))

    lane8 = lax.broadcasted_iota(jnp.int32, (8, 128), 1)

    def picked_lane(value, at):
        return jnp.sum(jnp.where(lane8 == at, value, 0.0), axis=1, keepdims=True)

    def finish(lse_parts, own_tile, got, places):
        lse, parts = shares(lse_parts)
        means, hits, lses = [], [], []
        for j, at in enumerate(places):
            mean = jnp.zeros((16, 128), F32)
            hit = jnp.zeros((16, 128), F32)
            for part, tile in zip(parts, [own_tile] + got):
                mean = mean + twice(picked_lane(part, at)) * tile(0, j).astype(F32)
                hit = hit + tile(1, j).astype(F32)
            means.append(mean)
            hits.append(hit)
            lses.append(picked_lane(lse, at))
        return means, hits, lses

    for d in range(1, NX):
        rcopy(flB.at[d - 1], flB.at[d - 1], lds.at[d - 1], ldr.at[d - 1], at_x(d)).wait_recv()
        rcopy(rx_b.at[d - 1], rx_b.at[d - 1], rds.at[d - 1], rdr.at[d - 1], at_x(d)).wait_recv()
    late = finish(
        [qlb[...]] + [flB[d - 1] for d in range(1, NX)],
        lambda n, j: q_b[x, n],
        [lambda n, j, d=d: rx_b[d - 1, n] for d in range(1, NX)],
        [8 * x],
    )
    for d in range(1, NZ):
        rcopy(flA.at[d - 1], flA.at[d - 1], lcs.at[d - 1], lcr.at[d - 1], at_z(d)).wait_recv()
        rcopy(rz_a.at[d - 1], rz_a.at[d - 1], rcs.at[d - 1], rcr.at[d - 1], at_z(d)).wait_recv()
    early = finish(
        [qla[...]] + [flA[d - 1] for d in range(1, NZ)],
        lambda n, j: q_a[z, n, j],
        [lambda n, j, d=d: rz_a[d - 1, n, j] for d in range(1, NZ)],
        [16 * z, 16 * z + 8],
    )
    means, hits, lses = [a + b for a, b in zip(early, late)]
    mean = jnp.concatenate([jnp.concatenate([v[:8], v[8:]], axis=1) for v in means], axis=0)
    hit = jnp.concatenate([jnp.concatenate([v[:8], v[8:]], axis=1) for v in hits], axis=0)
    squashed = jnp.tanh(feats[...].astype(F32) / scale)
    student = (scale * squashed).astype(BF16).astype(F32)
    grad_out[...] = (mean - hit) * (1.0 - squashed * squashed)
    column = jnp.concatenate(lses, axis=0) - jnp.sum(student * hit, axis=1, keepdims=True)
    loss_out[...] = jnp.sum(jnp.where(eye, column, 0.0), axis=0, keepdims=True)

    for copy in sends:
        copy.wait_send()


def body(features, scale_exponents, targets, centres):
    def dma(*shape):
        return pltpu.SemaphoreType.DMA(shape)

    vx, vz = [dma(NX - 1)] * 2, [dma(NZ - 1)] * 2
    loss, grad = pl.pallas_call(
        kernel,
        out_shape=(jax.ShapeDtypeStruct((1, 128), F32), jax.ShapeDtypeStruct((OWN, D), F32)),
        in_specs=[pl.BlockSpec(memory_space=pl.ANY)] * 4,
        out_specs=(pl.BlockSpec(memory_space=pltpu.VMEM), pl.BlockSpec(memory_space=pltpu.VMEM)),
        scratch_shapes=[
            pltpu.SMEM((D // QB,), jnp.int32),
            pltpu.SMEM((OWN,), jnp.int32),
            pltpu.VMEM((OWN, D), BF16),
            pltpu.VMEM((UNITS, HALF, D), BF16),
            pltpu.VMEM((NL, 2, 16, 128), BF16),
            pltpu.VMEM((NL, 16, 128), BF16),
            pltpu.VMEM((NL, 1, 128), jnp.int32),
            pltpu.VMEM((ROWS, D), BF16),
            pltpu.VMEM((ROWS, 128), jnp.int32),
            pltpu.VMEM((ROWS, 128), F32),
            pltpu.VMEM((ROWS, 128), F32),
            pltpu.VMEM((ROWS, D), F32),
            pltpu.VMEM((ROWS, D), F32),
            pltpu.VMEM((NL, 2, 16, 128), BF16),
            pltpu.VMEM((NL, 16, 128), BF16),
            pltpu.VMEM((NL, 2, 16, 128), BF16),
            pltpu.VMEM((NL, 16, 128), BF16),
            pltpu.VMEM((NX - 1, NZ, 2, 16, 128), BF16),
            pltpu.VMEM((NZ - 1, NX, 16, 128), BF16),
            pltpu.VMEM((NX, 8, 128), F32),
            pltpu.VMEM((NZ, 8, 128), F32),
            pltpu.VMEM((NX - 1, NZ, 2, 16, 128), BF16),
            pltpu.VMEM((NZ - 1, NX, 16, 128), BF16),
            pltpu.VMEM((NX - 1, 8, 128), F32),
            pltpu.VMEM((NZ - 1, 8, 128), F32),
            pltpu.VMEM((NZ, 2, 2, 16, 128), BF16),
            pltpu.VMEM((NX, 2, 16, 128), BF16),
            pltpu.VMEM((8, 128), F32),
            pltpu.VMEM((8, 128), F32),
            pltpu.VMEM((NZ - 1, 2, 2, 16, 128), BF16),
            pltpu.VMEM((NX - 1, 2, 16, 128), BF16),
            pltpu.VMEM((NZ - 1, 8, 128), F32),
            pltpu.VMEM((NX - 1, 8, 128), F32),
            dma(3),
            dma(2),
            dma(14),
            dma(UNITS),
            *vz, *vx, *vz, *vx, *vz, *vx,
            *vx, *vz, *vz, *vx,
            *vx, *vz, *vx, *vz, *vz, *vx,
        ],
        compiler_params=pltpu.CompilerParams(
            collective_id=0, has_side_effects=True, vmem_limit_bytes=60 * 1024 * 1024
        ),
    )(scale_exponents, targets, features, centres)
    return loss[0, :OWN], grad


def solution(mesh):
    placed = (P(("loop", "group"), None), P(), P(("loop", "group")), P(("loop", "group"), None))
    return jax.shard_map(
        body,
        mesh=mesh,
        in_specs=placed,
        out_specs=(P(("loop", "group")), P(("loop", "group"), None)),
        check_vma=False,
    )
```

time: 68.7 us -> 53.6 us (0.78)
  the two profiles are of different devices: /device:TPU:8 before, /device:TPU:1 now
where the time goes in v2:
time: 53.6 us; the launch traced here: 53.4 us
  Pallas kernels  50.3 us (94%)
  local copies, waits for them, and re-layouts  2.48 us (5%)
  between operations  0.65 us (1%)
    pallas_call x1, Pallas kernels, body(): pl.pallas_call(kernel, out_shape=(jax.ShapeDtypeStruct((1, 128), F32), ja...  50.3 us
    unnamed x3, local copies, waits for them, and re-layouts  1.97 us

profile of v2, /device:TPU:1, one launch (start us, length us, event | category | flops | bytes accessed | tf_op | source)
XLA Modules:
  0.0 53.4 jit_solution(12886712254933813418)
XLA Ops:
  0.6 50.3 %shard_map.59 = (f32[1,128]{1,0:T(1,128)}, f32[24,256]{1,0:T(8,128)}) custom-call(s32[8]{0:T(128)} %exps_hbm.1, s32[24]{0:T(128)} %tgts_hbm.1, bf16[24,256]{1,0:T(8,128)(2,1)} %feats_hbm.1, bf16[1024,256]{1,0:T(8,128)(2,1)} %cents.1), custom_call_target="tpu_custom_call" | custom-call | tf_op jit(solution)/shard_map/pallas_call | solution.py:401
  50.9 0.0 copy-start
  50.9 0.6 %copy-done = f32[1,128]{1,0:T(1,128)S(1)} copy-done((f32[1,128]{1,0:T(1,128)S(1)}, f32[1,128]{1,0:T(1,128)}, u32[]{:S(2)}) %copy-start) | copy-done | bytes 536
  51.6 0.5 slice_bitcast_fusion
  52.1 1.3 %copy.7 = f32[24,256]{1,0:T(8,128)} copy(f32[24,256]{1,0:T(8,128)} %get-tuple-element.9) | data formatting | bytes 49152
Async XLA Ops:
  50.9 0.6 %copy-start = (f32[1,128]{1,0:T(1,128)S(1)}, f32[1,128]{1,0:T(1,128)}, u32[]{:S(2)}) copy-start(f32[1,128]{1,0:T(1,128)} %get-tuple-element.4) | copy-start | bytes 1540

commit v3 on v0

v3 whole, which is shorter than its diff:
```python
import jax
import jax.numpy as jnp
from jax import lax
from jax.experimental import pallas as pl
from jax.experimental.pallas import tpu as pltpu
from jax.sharding import PartitionSpec as P

F32 = jnp.float32
BF16 = jnp.bfloat16
MESH = pl.DeviceIdType.MESH

NX, NY, NZ = 4, 4, 8
NL = NX * NZ
D = 256
QB = 32
OWN = 24
ROWS = OWN * NL
HALF = 512
UNITS = 16
PART = 8 * NL
FIRST, SECOND = (NZ, NX, NZ), (NX, NZ, NX)
TILE = (0, 2, 1)


def rcopy(src, dst, send, recv, device):
    return pltpu.make_async_remote_copy(
        src_ref=src, dst_ref=dst, send_sem=send, recv_sem=recv, device_id=device, device_id_type=MESH
    )


def joined(tiles):
    count = tiles.shape[0]
    low = tiles[:, :8].reshape(count * 8, 128)
    high = tiles[:, 8:].reshape(count * 8, 128)
    return jnp.concatenate([low, high], axis=1)


def parted(rows):
    count = rows.shape[0] // 8
    low = rows[:, :128].reshape(count, 8, 128)
    high = rows[:, 128:].reshape(count, 8, 128)
    return jnp.concatenate([low, high], axis=1)


def shares(parts):
    top = parts[0]
    for part in parts[1:]:
        top = jnp.maximum(top, part)
    powers = [jnp.exp(part - top) for part in parts]
    total = powers[0]
    for power in powers[1:]:
        total = total + power
    return top + jnp.log(total), [power / total for power in powers]


def twice(column):
    wide = jnp.broadcast_to(column, (8, 128))
    return jnp.concatenate([wide, wide], axis=0)


def kernel(
    exps_hbm, tgts_hbm, feats_hbm, cents, loss_out, grad_out,
    exps, tgts, feats, cbuf, tgb, sbf, tcol, m, l, acc, t, *rest
):
    rest = list(rest)

    def take(count):
        out, rest[:count] = rest[:count], []
        return out

    ag, pk, ht, ls, rx, rht, rls, q, qls, rz, fls, psend, precv, hsend, hrecv = [take(3) for _ in range(15)]
    in_sem, c_sem, ring_send, unit_recv, tsend, trecv = rest
    loop = lax.axis_index("loop")
    group = lax.axis_index("group")
    x, z = loop // NZ, loop % NZ
    y, core = group // 2, group % 2
    other = 1 - core

    def chip(dx, dy, c):
        return (((x + dx + NX) % NX) * NZ + z, ((y + dy + NY) % NY) * 2 + c)

    def along_x(d):
        return chip(d, 0, core)

    def along_z(d):
        return (x * NZ + (z + d) % NZ, group)

    sibling = chip(0, 0, other)
    up, down = chip(0, 1, core), chip(0, -1, core)
    barrier = pltpu.get_barrier_semaphore()
    partners = [along_z(d) for d in range(1, NZ)] + [along_x(d) for d in range(1, NX)]
    partners += [sibling, up, down]
    for partner in partners:
        pl.semaphore_signal(barrier, inc=1, device_id=partner, device_id_type=MESH)

    small = [
        pltpu.make_async_copy(exps_hbm, exps, in_sem.at[0]),
        pltpu.make_async_copy(tgts_hbm, tgts, in_sem.at[1]),
        pltpu.make_async_copy(feats_hbm, feats, in_sem.at[2]),
    ]
    own = [
        pltpu.make_async_copy(cents.at[pl.ds(h * HALF, HALF)], cbuf.at[h], c_sem.at[h]) for h in range(2)
    ]
    for copy in small + own:
        copy.start()
    for copy in small:
        copy.wait()

    hop1 = (along_z, along_x, along_z)
    hop2 = (along_x, along_z, along_x)
    here1, here2 = (z, x, z), (x, z, x)

    block = lax.broadcasted_iota(jnp.int32, (1, D), 1) // QB
    scale = jnp.zeros((1, D), F32)
    for b in range(D // QB):
        e = exps[b]
        power = jnp.where(e < 0, 0.5, jnp.where(e < 1, 1.0, jnp.where(e < 2, 2.0, 4.0)))
        scale = jnp.where(block == b, power, scale)
    squashed = jnp.tanh(feats[...].astype(F32) / scale)
    student = (scale * squashed).astype(BF16).astype(F32)
    tiles = parted(student).astype(BF16)
    for p in range(3):
        ag[p][here2[p] * FIRST[p] + here1[p]] = tiles[TILE[p]]
    lane = lax.broadcasted_iota(jnp.int32, (1, 128), 1)
    ids = jnp.zeros((1, 128), jnp.int32)
    for i in range(OWN):
        ids = jnp.where(lane == i, tgts[i], ids)
    tgb[loop] = ids

    pl.semaphore_wait(barrier, len(partners))

    sends = []

    def go(copy):
        copy.start()
        sends.append(copy)

    def ag1(p, d, slot):
        ref = ag[p].at[slot]
        return rcopy(ref, ref, psend[p].at[d - 1], precv[p].at[d - 1], hop1[p](d))

    def ag2(p, d, place):
        ref = ag[p].at[pl.ds(place * FIRST[p], FIRST[p])]
        sem = FIRST[p] - 2 + d
        return rcopy(ref, ref, psend[p].at[sem], precv[p].at[sem], hop2[p](d))

    def behind(p, axis, d):
        count = (FIRST, SECOND)[axis][p]
        return ((here1, here2)[axis][p] + count - d) % count

    for p in range(3):
        for d in range(1, FIRST[p]):
            go(ag1(p, d, here2[p] * FIRST[p] + here1[p]))
        if p == 0:
            for d in range(1, NZ):
                go(rcopy(tgb.at[loop], tgb.at[loop], tsend.at[d - 1], trecv.at[d - 1], along_z(d)))

    for copy in own:
        copy.wait()

    quarter = HALF // 2
    halves = (pl.ds(0, quarter), pl.ds(quarter, quarter))
    rings = ((0, 4, up, 12), (1, 5, down, 13))

    def ring(n, source, target, half, device):
        return rcopy(
            cbuf.at[source, halves[half]], cbuf.at[target, halves[half]],
            ring_send.at[n], unit_recv.at[2 * target + half], device,
        )

    def whole(n, source, target, device=sibling):
        return rcopy(cbuf.at[source], cbuf.at[target], ring_send.at[n], unit_recv.at[2 * target], device)

    for half in range(2):
        for n, (source, target, device, _) in enumerate(rings):
            go(ring(2 * half + n, source, target, half, device))
    go(whole(4, 0, 2))
    go(whole(5, 1, 3))
    go(whole(6, 1, 6, up))
    go(whole(7, 0, 7, down))

    for p in range(3):
        for d in range(1, FIRST[p]):
            ag1(p, d, here2[p] * FIRST[p] + behind(p, 0, d)).wait_recv()
        for d in range(1, SECOND[p]):
            go(ag2(p, d, here2[p]))
        if p == 0:
            for d in range(1, NZ):
                slot = tgb.at[x * NZ + (z + NZ - d) % NZ]
                rcopy(slot, slot, tsend.at[d - 1], trecv.at[d - 1], along_z(d)).wait_recv()
            for d in range(1, NX):
                line = tgb.at[pl.ds(x * NZ, NZ)]
                sem = NZ - 2 + d
                go(rcopy(line, line, tsend.at[sem], trecv.at[sem], along_x(d)))

    def arrive(*units):
        for u in units:
            whole(0, u, u).wait_recv()

    def rows_of(p):
        for d in range(1, SECOND[p]):
            ag2(p, d, behind(p, 1, d)).wait_recv()
        sbf[p * PART : (p + 1) * PART, :] = joined(ag[p][...].astype(F32)).astype(BF16)

    eye = lax.broadcasted_iota(jnp.int32, (OWN, 128), 0) == lax.broadcasted_iota(jnp.int32, (OWN, 128), 1)
    lanes = lax.broadcasted_iota(jnp.int32, (1, 128), 1)
    block16 = lax.broadcasted_iota(jnp.int32, (8, 128), 1) // 16

    def pick(pieces, first=False):
        rows = pl.ds(0, ROWS)
        cb = jnp.concatenate([cbuf[u, at : at + size] for u, at, size, _ in pieces], axis=0)
        hits = []
        for _, _, size, base in pieces:
            where = tcol[rows, :] - base
            for k in range(size // 128):
                hits.append(jnp.where(where == lanes + k * 128, 1.0, 0.0).astype(BF16))
        hit = jnp.dot(jnp.concatenate(hits, axis=1), cb, preferred_element_type=F32)
        t[rows, :] = hit if first else t[rows, :] + hit

    def chunk(pieces, first=False, picks=True):
        rows = pl.ds(0, ROWS)
        cb = jnp.concatenate([cbuf[u, at : at + size] for u, at, size, _ in pieces], axis=0)
        logits = lax.dot_general(sbf[rows, :], cb, (((1,), (1,)), ((), ())), preferred_element_type=F32)
        new = jnp.max(logits, axis=1, keepdims=True)
        if first:
            new = jnp.broadcast_to(new, (ROWS, 128))
            total = jnp.zeros((ROWS, 128), F32)
        else:
            old = m[rows, :]
            new = jnp.maximum(old, new)
            fade = jnp.exp(old - new)
            total = l[rows, :] * fade
        m[rows, :] = new
        weights = []
        for k in range(cb.shape[0] // 128):
            w = jnp.exp(logits[:, k * 128 : (k + 1) * 128] - new)
            total = total + w
            weights.append(w.astype(BF16))
        l[rows, :] = total
        mean = jnp.dot(jnp.concatenate(weights, axis=1), cb, preferred_element_type=F32)
        if first:
            acc[rows, :] = mean
        else:
            acc[rows, :] = acc[rows, :] * jnp.concatenate([fade, fade], axis=1) + mean
        if picks:
            pick(pieces, first)

    def piece(u, dy, c, h, half=None):
        base = (loop * 2 * NY + ((y + dy) % NY) * 2 + c) * (2 * HALF) + h * HALF
        return (u, 0, HALF, base) if half is None else (u, half * quarter, quarter, base + half * quarter)

    quads = [
        [piece(0, 0, core, 0), piece(1, 0, core, 1), piece(2, 0, other, 0), piece(3, 0, other, 1)],
        [piece(4, 3, core, 0), piece(5, 1, core, 1), piece(6, 3, core, 1), piece(7, 1, core, 0)],
        [piece(8, 3, other, 0), piece(9, 1, other, 1), piece(10, 3, other, 1), piece(11, 1, other, 0)],
    ]
    ends = [
        [piece(12, 2, core, 0, k), piece(13, 2, core, 1, k), piece(14, 2, other, 0, k), piece(15, 2, other, 1, k)]
        for k in range(2)
    ]

    def rs2(p, d, place, which):
        n1 = FIRST[p]
        sem = n1 + SECOND[p] - 3 + d
        make = [
            lambda: rcopy(
                pk[p].at[pl.ds(place * n1, n1)], rx[p].at[d - 1],
                psend[p].at[sem], precv[p].at[sem], hop2[p](d),
            ),
            lambda: rcopy(
                ht[p].at[pl.ds(place * n1, n1)], rht[p].at[d - 1],
                hsend[p].at[d - 1], hrecv[p].at[d - 1], hop2[p](d),
            ),
            lambda: rcopy(
                ls[p].at[place], rls[p].at[d - 1],
                psend[p].at[sem + SECOND[p] - 1], precv[p].at[sem + SECOND[p] - 1], hop2[p](d),
            ),
        ]
        return make[which]()

    def rs1(p, d, place):
        n1 = FIRST[p]
        sem = n1 + 3 * SECOND[p] - 5 + d
        return [
            rcopy(q[p].at[place], rz[p].at[d - 1], psend[p].at[sem], precv[p].at[sem], hop1[p](d)),
            rcopy(qls[p], fls[p].at[d - 1], psend[p].at[sem + n1 - 1], precv[p].at[sem + n1 - 1], hop1[p](d)),
        ]

    def send_picks(p):
        ht[p][...] = parted(t[p * PART : (p + 1) * PART, :]).astype(BF16)
        for d in range(1, SECOND[p]):
            go(rs2(p, d, (here2[p] + d) % SECOND[p], 1))

    def send_part(p):
        n1, n2 = FIRST[p], SECOND[p]
        rows = pl.ds(p * PART, PART)
        total = jnp.sum(l[rows, :], axis=1, keepdims=True)
        l[rows, :] = m[rows, :] + jnp.log(total)
        pk[p][...] = parted(acc[rows, :] * (1.0 / total)).astype(BF16)
        for k in range(n2):
            out = jnp.zeros((8, 128), F32)
            for j in range(n1):
                at = p * PART + 8 * (k * n1 + j)
                out = jnp.where(block16 == j, l[at : at + 8, :], out)
            ls[p][k] = out
        for d in range(1, n2):
            go(rs2(p, d, (here2[p] + d) % n2, 0))
            go(rs2(p, d, (here2[p] + d) % n2, 2))

    def merge_part(p):
        n1, n2 = FIRST[p], SECOND[p]
        for d in range(1, n2):
            for which in range(3):
                rs2(p, d, here2[p], which).wait_recv()
        lse, parts = shares([ls[p][here2[p]]] + [rls[p][d - 1] for d in range(1, n2)])
        qls[p][...] = lse
        for k in range(n1):
            got = [pk[p][here2[p] * n1 + k]] + [rx[p][d - 1, k] for d in range(1, n2)]
            mean = jnp.zeros((16, 128), F32)
            for part, tile in zip(parts, got):
                mean = mean + twice(part[:, 16 * k : 16 * k + 1]) * tile.astype(F32)
            q[p][k, 0] = mean.astype(BF16)
        hit = ht[p][pl.ds(here2[p] * n1, n1)]
        for d in range(1, n2):
            hit = hit + rht[p][d - 1]
        q[p][:, 1] = hit
        for d in range(1, n1):
            for copy in rs1(p, d, (here1[p] + d) % n1):
                go(copy)

    lane8 = lax.broadcasted_iota(jnp.int32, (8, 128), 1)

    def finish_part(p):
        n1 = FIRST[p]
        for d in range(1, n1):
            for copy in rs1(p, d, here1[p]):
                copy.wait_recv()
        lse, parts = shares([qls[p][...]] + [fls[p][d - 1] for d in range(1, n1)])

        def picked_lane(value):
            return jnp.sum(jnp.where(lane8 == 16 * here1[p], value, 0.0), axis=1, keepdims=True)

        mean = jnp.zeros((16, 128), F32)
        hit = jnp.zeros((16, 128), F32)
        for part, tile in zip(parts, [q[p][here1[p]]] + [rz[p][d - 1] for d in range(1, n1)]):
            mean = mean + twice(picked_lane(part)) * tile[0].astype(F32)
            hit = hit + tile[1].astype(F32)
        wide = [jnp.concatenate([v[:8], v[8:]], axis=1) for v in (mean, hit)]
        return wide + [picked_lane(lse)]

    rows_of(0)
    for d in range(1, NX):
        line = tgb.at[pl.ds(((x + NX - d) % NX) * NZ, NZ)]
        sem = NZ - 2 + d
        rcopy(line, line, tsend.at[sem], trecv.at[sem], along_x(d)).wait_recv()
    for k in range(NL):
        row = tgb[k].astype(F32)
        column = jnp.sum(jnp.where(eye, row, 0.0), axis=1, keepdims=True).astype(jnp.int32)
        for p in range(3):
            slot = (k % NZ) * NX + k // NZ if p == 1 else k
            at = p * PART + 8 * slot
            tcol[at : at + 8, :] = jnp.broadcast_to(column[8 * TILE[p] : 8 * TILE[p] + 8], (8, 128))
    def pass_on(half):
        for n, (_, target, device, last) in enumerate(rings):
            ring(0, target, target, half, device).wait_recv()
            go(ring(8 + 2 * half + n, target, last, half, device))

    rows_of(1)
    rows_of(2)
    pass_on(0)
    arrive(2, 3)
    chunk(quads[0], True)
    pass_on(1)
    go(whole(12, 4, 8))
    go(whole(13, 5, 9))
    arrive(6, 7)
    go(whole(14, 6, 10))
    go(whole(15, 7, 11))
    chunk(quads[1])
    for half in range(2):
        for u in (12, 13):
            ring(0, u, u, half, sibling).wait_recv()
            go(ring(4 + 2 * half + u, u, u + 2, half, sibling))
        if half == 0:
            arrive(8, 9, 10, 11)
            chunk(quads[2])
    for half in range(2):
        for u in (14, 15):
            ring(0, u, u, half, sibling).wait_recv()
        if half == 0:
            chunk(ends[0])
    pick(ends[1])
    for p in range(3):
        send_picks(p)
    chunk(ends[1], False, False)
    for p in (0, 2, 1):
        send_part(p)
    merge_part(0)
    merge_part(2)
    merge_part(1)
    done = [finish_part(0), finish_part(1), finish_part(2)]
    mean, hit, lse = [jnp.concatenate([done[0][n], done[2][n], done[1][n]], axis=0) for n in range(3)]
    squashed = jnp.tanh(feats[...].astype(F32) / scale)
    student = (scale * squashed).astype(BF16).astype(F32)
    grad_out[...] = (mean - hit) * (1.0 - squashed * squashed)
    column = lse - jnp.sum(student * hit, axis=1, keepdims=True)
    loss_out[...] = jnp.sum(jnp.where(eye, column, 0.0), axis=0, keepdims=True)

    for copy in sends:
        copy.wait_send()


def body(features, scale_exponents, targets, centres):
    def dma(*shape):
        return pltpu.SemaphoreType.DMA(shape)

    def per_part(make):
        return [make(FIRST[p], SECOND[p]) for p in range(3)]

    loss, grad = pl.pallas_call(
        kernel,
        out_shape=(jax.ShapeDtypeStruct((1, 128), F32), jax.ShapeDtypeStruct((OWN, D), F32)),
        in_specs=[pl.BlockSpec(memory_space=pl.ANY)] * 4,
        out_specs=(pl.BlockSpec(memory_space=pltpu.VMEM), pl.BlockSpec(memory_space=pltpu.VMEM)),
        scratch_shapes=[
            pltpu.SMEM((D // QB,), jnp.int32),
            pltpu.SMEM((OWN,), jnp.int32),
            pltpu.VMEM((OWN, D), BF16),
            pltpu.VMEM((UNITS, HALF, D), BF16),
            pltpu.VMEM((NL, 1, 128), jnp.int32),
            pltpu.VMEM((ROWS, D), BF16),
            pltpu.VMEM((ROWS, 128), jnp.int32),
            pltpu.VMEM((ROWS, 128), F32),
            pltpu.VMEM((ROWS, 128), F32),
            pltpu.VMEM((ROWS, D), F32),
            pltpu.VMEM((ROWS, D), F32),
            *per_part(lambda a, b: pltpu.VMEM((NL, 16, 128), BF16)),
            *per_part(lambda a, b: pltpu.VMEM((NL, 16, 128), BF16)),
            *per_part(lambda a, b: pltpu.VMEM((NL, 16, 128), BF16)),
            *per_part(lambda a, b: pltpu.VMEM((b, 8, 128), F32)),
            *per_part(lambda a, b: pltpu.VMEM((b - 1, a, 16, 128), BF16)),
            *per_part(lambda a, b: pltpu.VMEM((b - 1, a, 16, 128), BF16)),
            *per_part(lambda a, b: pltpu.VMEM((b - 1, 8, 128), F32)),
            *per_part(lambda a, b: pltpu.VMEM((a, 2, 16, 128), BF16)),
            *per_part(lambda a, b: pltpu.VMEM((8, 128), F32)),
            *per_part(lambda a, b: pltpu.VMEM((a - 1, 2, 16, 128), BF16)),
            *per_part(lambda a, b: pltpu.VMEM((a - 1, 8, 128), F32)),
            *per_part(lambda a, b: dma(3 * (a + b - 2))),
            *per_part(lambda a, b: dma(3 * (a + b - 2))),
            *per_part(lambda a, b: dma(b - 1)),
            *per_part(lambda a, b: dma(b - 1)),
            dma(3),
            dma(2),
            dma(20),
            dma(2 * UNITS),
            dma(NX + NZ - 2),
            dma(NX + NZ - 2),
        ],
        compiler_params=pltpu.CompilerParams(
            collective_id=0, has_side_effects=True, vmem_limit_bytes=60 * 1024 * 1024
        ),
    )(scale_exponents, targets, features, centres)
    return loss[0, :OWN], grad


def solution(mesh):
    placed = (P(("loop", "group"), None), P(), P(("loop", "group")), P(("loop", "group"), None))
    return jax.shard_map(
        body,
        mesh=mesh,
        in_specs=placed,
        out_specs=(P(("loop", "group")), P(("loop", "group"), None)),
        check_vma=False,
    )
```

time: 729 us -> 53 us (0.07)
  waiting for transfers between devices: 432 us -> 0 us
  blocking collectives: 112 us -> 0 us
  matrix products: 57.3 us -> 0 us
  local copies, waits for them, and re-layouts: 55.4 us -> 2.48 us
  Pallas kernels: 0 us -> 49.7 us
  other arithmetic: 24 us -> 0 us
  starting transfers between devices: 23.2 us -> 0 us
  between operations: 15.5 us -> 0.65 us
    ppermute x224 -> x0, waiting for transfers between devices: 406 us -> none  [from_behind(): return lax.ppermute(value, axis, pairs)]
    unnamed x2 -> x0, blocking collectives: 97 us -> none
    dot_general x64 -> x0, matrix products: 57.3 us -> none  [the longest x32 46.7 us: visit_shard(): lax.dot_general(block_rows, centres, (((1,), (1,)), ((), ())), preferred_...]
    pallas_call x0 -> x1, Pallas kernels: none -> 49.7 us  [body(): pl.pallas_call(kernel, out_shape=(jax.ShapeDtypeStruct((1, 128), F32), ja...]
    gather x32 -> x0, local copies, waits for them, and re-layouts: 32.1 us -> none  [visit_shard(): picked = jnp.take(centres, jnp.clip(local_ids, 0, shard_rows - 1), axis=0)]
    reduce_scatter x1 -> x0, waiting for transfers between devices: 25.6 us -> none  [body(): lax.psum_scatter(partial_grad.astype(jnp.bfloat16), 'group', scatter_dime...]
    ppermute x224 -> x0, starting transfers between devices: 23.2 us -> none  [from_behind(): return lax.ppermute(value, axis, pairs)]
    while x160 -> x0, local copies, waits for them, and re-layouts: 20.5 us -> none
  transfers between devices with their start and end apart: 225 -> 0, of which waited for: 85 -> 0; matrix products, arithmetic and copies ran while one was open for 15% -> 0% of each run, Pallas kernels for 0% -> 0%
where the time goes in v3:
time: 53 us; the launch traced here: 52.9 us
  Pallas kernels  49.7 us (94%)
  local copies, waits for them, and re-layouts  2.48 us (5%)
  between operations  0.65 us (1%)
    pallas_call x1, Pallas kernels, body(): pl.pallas_call(kernel, out_shape=(jax.ShapeDtypeStruct((1, 128), F32), ja...  49.7 us
    unnamed x3, local copies, waits for them, and re-layouts  1.97 us

profile of v3, /device:TPU:1, one launch (start us, length us, event | category | flops | bytes accessed | tf_op | source)
XLA Modules:
  0.0 52.9 jit_solution(1987842136553316447)
XLA Ops:
  0.6 49.7 %shard_map.59 = (f32[1,128]{1,0:T(1,128)}, f32[24,256]{1,0:T(8,128)}) custom-call(s32[8]{0:T(128)} %exps_hbm.1, s32[24]{0:T(128)} %tgts_hbm.1, bf16[24,256]{1,0:T(8,128)(2,1)} %feats_hbm.1, bf16[1024,256]{1,0:T(8,128)(2,1)} %cents.1), custom_call_target="tpu_custom_call" | custom-call | tf_op jit(solution)/shard_map/pallas_call | solution.py:420
  50.4 0.0 copy-start
  50.4 0.6 %copy-done = f32[1,128]{1,0:T(1,128)S(1)} copy-done((f32[1,128]{1,0:T(1,128)S(1)}, f32[1,128]{1,0:T(1,128)}, u32[]{:S(2)}) %copy-start) | copy-done | bytes 536
  51.0 0.5 slice_bitcast_fusion
  51.5 1.3 %copy.7 = f32[24,256]{1,0:T(8,128)} copy(f32[24,256]{1,0:T(8,128)} %get-tuple-element.9) | data formatting | bytes 49152
Async XLA Ops:
  50.4 0.6 %copy-start = (f32[1,128]{1,0:T(1,128)S(1)}, f32[1,128]{1,0:T(1,128)}, u32[]{:S(2)}) copy-start(f32[1,128]{1,0:T(1,128)} %get-tuple-element.4) | copy-start | bytes 1540

commit v4 on v3

--- a/solution.py
+++ b/solution.py
@@ -68,7 +68,7 @@
         out, rest[:count] = rest[:count], []
         return out
 
-    ag, pk, ht, ls, rx, rht, rls, q, qls, rz, fls, psend, precv, hsend, hrecv = [take(3) for _ in range(15)]
+    ag, pk, ht, ls, rx, rht, rls, q, qh, qls, rz, rzh, fls, psend, precv, hsend, hrecv, fsend, frecv = [take(3) for _ in range(19)]
     in_sem, c_sem, ring_send, unit_recv, tsend, trecv = rest
     loop = lax.axis_index("loop")
     group = lax.axis_index("group")
@@ -204,7 +204,8 @@
 
     eye = lax.broadcasted_iota(jnp.int32, (OWN, 128), 0) == lax.broadcasted_iota(jnp.int32, (OWN, 128), 1)
     lanes = lax.broadcasted_iota(jnp.int32, (1, 128), 1)
-    block16 = lax.broadcasted_iota(jnp.int32, (8, 128), 1) // 16
+    block8 = lax.broadcasted_iota(jnp.int32, (8, 128), 1) // 8
+    shift = (0, 0, NZ)
 
     def pick(pieces, first=False):
         rows = pl.ds(0, ROWS)
@@ -278,13 +279,16 @@
         ]
         return make[which]()
 
-    def rs1(p, d, place):
+    def rs1(p, d, place, which):
         n1 = FIRST[p]
         sem = n1 + 3 * SECOND[p] - 5 + d
-        return [
-            rcopy(q[p].at[place], rz[p].at[d - 1], psend[p].at[sem], precv[p].at[sem], hop1[p](d)),
-            rcopy(qls[p], fls[p].at[d - 1], psend[p].at[sem + n1 - 1], precv[p].at[sem + n1 - 1], hop1[p](d)),
+        far = sem + n1 - 1
+        make = [
+            lambda: rcopy(q[p].at[place], rz[p].at[d - 1], psend[p].at[sem], precv[p].at[sem], hop1[p](d)),
+            lambda: rcopy(qh[p].at[place], rzh[p].at[d - 1], fsend[p].at[d - 1], frecv[p].at[d - 1], hop1[p](d)),
+            lambda: rcopy(qls[p], fls[p].at[d - 1], psend[p].at[far], precv[p].at[far], hop1[p](d)),
         ]
+        return make[which]()
 
     def send_picks(p):
         ht[p][...] = parted(t[p * PART : (p + 1) * PART, :]).astype(BF16)
@@ -301,52 +305,66 @@
             out = jnp.zeros((8, 128), F32)
             for j in range(n1):
                 at = p * PART + 8 * (k * n1 + j)
-                out = jnp.where(block16 == j, l[at : at + 8, :], out)
+                out = jnp.where(block8 == shift[p] + j, l[at : at + 8, :], out)
             ls[p][k] = out
         for d in range(1, n2):
             go(rs2(p, d, (here2[p] + d) % n2, 0))
             go(rs2(p, d, (here2[p] + d) % n2, 2))
 
+    def merge_picks(p):
+        n1, n2 = FIRST[p], SECOND[p]
+        for d in range(1, n2):
+            rs2(p, d, here2[p], 1).wait_recv()
+        hit = ht[p][pl.ds(here2[p] * n1, n1)]
+        for d in range(1, n2):
+            hit = hit + rht[p][d - 1]
+        qh[p][...] = hit
+        for d in range(1, n1):
+            go(rs1(p, d, (here1[p] + d) % n1, 1))
+
     def merge_part(p):
         n1, n2 = FIRST[p], SECOND[p]
         for d in range(1, n2):
-            for which in range(3):
-                rs2(p, d, here2[p], which).wait_recv()
+            rs2(p, d, here2[p], 0).wait_recv()
+            rs2(p, d, here2[p], 2).wait_recv()
         lse, parts = shares([ls[p][here2[p]]] + [rls[p][d - 1] for d in range(1, n2)])
-        qls[p][...] = lse
+        qls[p][...] = jnp.where(block8 < NZ, qls[0][...], lse) if p == 2 else lse
         for k in range(n1):
             got = [pk[p][here2[p] * n1 + k]] + [rx[p][d - 1, k] for d in range(1, n2)]
             mean = jnp.zeros((16, 128), F32)
             for part, tile in zip(parts, got):
-                mean = mean + twice(part[:, 16 * k : 16 * k + 1]) * tile.astype(F32)
-            q[p][k, 0] = mean.astype(BF16)
-        hit = ht[p][pl.ds(here2[p] * n1, n1)]
-        for d in range(1, n2):
-            hit = hit + rht[p][d - 1]
-        q[p][:, 1] = hit
+                at = 8 * (shift[p] + k)
+                mean = mean + twice(part[:, at : at + 1]) * tile.astype(F32)
+            q[p][k] = mean.astype(BF16)
         for d in range(1, n1):
-            for copy in rs1(p, d, (here1[p] + d) % n1):
-                go(copy)
+            go(rs1(p, d, (here1[p] + d) % n1, 0))
+            if p != 0:
+                go(rs1(p, d, (here1[p] + d) % n1, 2))
 
     lane8 = lax.broadcasted_iota(jnp.int32, (8, 128), 1)
 
-    def finish_part(p):
+    def finish_part(p, lse, parts):
         n1 = FIRST[p]
         for d in range(1, n1):
-            for copy in rs1(p, d, here1[p]):
-                copy.wait_recv()
-        lse, parts = shares([qls[p][...]] + [fls[p][d - 1] for d in range(1, n1)])
+            rs1(p, d, here1[p], 0).wait_recv()
+            rs1(p, d, here1[p], 1).wait_recv()
 
         def picked_lane(value):
-            return jnp.sum(jnp.where(lane8 == 16 * here1[p], value, 0.0), axis=1, keepdims=True)
+            return jnp.sum(jnp.where(lane8 == 8 * (shift[p] + here1[p]), value, 0.0), axis=1, keepdims=True)
 
         mean = jnp.zeros((16, 128), F32)
-        hit = jnp.zeros((16, 128), F32)
         for part, tile in zip(parts, [q[p][here1[p]]] + [rz[p][d - 1] for d in range(1, n1)]):
-            mean = mean + twice(picked_lane(part)) * tile[0].astype(F32)
-            hit = hit + tile[1].astype(F32)
-        wide = [jnp.concatenate([v[:8], v[8:]], axis=1) for v in (mean, hit)]
+            mean = mean + twice(picked_lane(part)) * tile.astype(F32)
+        hit = qh[p][here1[p]]
+        for d in range(1, n1):
+            hit = hit + rzh[p][d - 1]
+        wide = [jnp.concatenate([v[:8], v[8:]], axis=1) for v in (mean, hit.astype(F32))]
         return wide + [picked_lane(lse)]
+
+    def last_shares(p):
+        for d in range(1, FIRST[p]):
+            rs1(p, d, here1[p], 2).wait_recv()
+        return shares([qls[p][...]] + [fls[p][d - 1] for d in range(1, FIRST[p])])
 
     rows_of(0)
     for d in range(1, NX):
@@ -390,15 +408,21 @@
         if half == 0:
             chunk(ends[0])
     pick(ends[1])
+    early = list(sends)
+    sends.clear()
     for p in range(3):
         send_picks(p)
     chunk(ends[1], False, False)
     for p in (0, 2, 1):
         send_part(p)
-    merge_part(0)
-    merge_part(2)
-    merge_part(1)
-    done = [finish_part(0), finish_part(1), finish_part(2)]
+    for copy in early:
+        copy.wait_send()
+    for p in (0, 2, 1):
+        merge_picks(p)
+    for p in (0, 2, 1):
+        merge_part(p)
+    both = last_shares(2)
+    done = [finish_part(0, *both), finish_part(1, *last_shares(1)), finish_part(2, *both)]
     mean, hit, lse = [jnp.concatenate([done[0][n], done[2][n], done[1][n]], axis=0) for n in range(3)]
     squashed = jnp.tanh(feats[...].astype(F32) / scale)
     student = (scale * squashed).astype(BF16).astype(F32)
@@ -441,14 +465,18 @@
             *per_part(lambda a, b: pltpu.VMEM((b - 1, a, 16, 128), BF16)),
             *per_part(lambda a, b: pltpu.VMEM((b - 1, a, 16, 128), BF16)),
             *per_part(lambda a, b: pltpu.VMEM((b - 1, 8, 128), F32)),
-            *per_part(lambda a, b: pltpu.VMEM((a, 2, 16, 128), BF16)),
+            *per_part(lambda a, b: pltpu.VMEM((a, 16, 128), BF16)),
+            *per_part(lambda a, b: pltpu.VMEM((a, 16, 128), BF16)),
             *per_part(lambda a, b: pltpu.VMEM((8, 128), F32)),
-            *per_part(lambda a, b: pltpu.VMEM((a - 1, 2, 16, 128), BF16)),
+            *per_part(lambda a, b: pltpu.VMEM((a - 1, 16, 128), BF16)),
+            *per_part(lambda a, b: pltpu.VMEM((a - 1, 16, 128), BF16)),
             *per_part(lambda a, b: pltpu.VMEM((a - 1, 8, 128), F32)),
             *per_part(lambda a, b: dma(3 * (a + b - 2))),
             *per_part(lambda a, b: dma(3 * (a + b - 2))),
             *per_part(lambda a, b: dma(b - 1)),
             *per_part(lambda a, b: dma(b - 1)),
+            *per_part(lambda a, b: dma(a - 1)),
+            *per_part(lambda a, b: dma(a - 1)),
             dma(3),
             dma(2),
             dma(20),

time: 53 us -> 52.7 us (level)
  no operation moved by 1% of the time
where the time goes in v4:
time: 52.7 us; the launch traced here: 52.5 us
  Pallas kernels  49.4 us (94%)
  local copies, waits for them, and re-layouts  2.48 us (5%)
  between operations  0.65 us (1%)
    pallas_call x1, Pallas kernels, body(): pl.pallas_call(kernel, out_shape=(jax.ShapeDtypeStruct((1, 128), F32), ja...  49.4 us
    unnamed x3, local copies, waits for them, and re-layouts  1.97 us

profile of v4, /device:TPU:1, one launch (start us, length us, event | category | flops | bytes accessed | tf_op | source)
XLA Modules:
  0.0 52.5 jit_solution(2108153411903064873)
XLA Ops:
  0.6 49.4 %shard_map.59 = (f32[1,128]{1,0:T(1,128)}, f32[24,256]{1,0:T(8,128)}) custom-call(s32[8]{0:T(128)} %exps_hbm.1, s32[24]{0:T(128)} %tgts_hbm.1, bf16[24,256]{1,0:T(8,128)(2,1)} %feats_hbm.1, bf16[1024,256]{1,0:T(8,128)(2,1)} %cents.1), custom_call_target="tpu_custom_call" | custom-call | tf_op jit(solution)/shard_map/pallas_call | solution.py:444
  50.0 0.0 copy-start
  50.0 0.6 %copy-done = f32[1,128]{1,0:T(1,128)S(1)} copy-done((f32[1,128]{1,0:T(1,128)S(1)}, f32[1,128]{1,0:T(1,128)}, u32[]{:S(2)}) %copy-start) | copy-done | bytes 536
  50.6 0.5 slice_bitcast_fusion
  51.2 1.3 %copy.7 = f32[24,256]{1,0:T(8,128)} copy(f32[24,256]{1,0:T(8,128)} %get-tuple-element.9) | data formatting | bytes 49152
Async XLA Ops:
  50.0 0.6 %copy-start = (f32[1,128]{1,0:T(1,128)S(1)}, f32[1,128]{1,0:T(1,128)}, u32[]{:S(2)}) copy-start(f32[1,128]{1,0:T(1,128)} %get-tuple-element.4) | copy-start | bytes 1540

commit v5 on v4

--- a/solution.py
+++ b/solution.py
@@ -410,13 +410,16 @@
     pick(ends[1])
     early = list(sends)
     sends.clear()
-    for p in range(3):
+    for p in (0, 2, 1):
         send_picks(p)
     chunk(ends[1], False, False)
     for p in (0, 2, 1):
         send_part(p)
     for copy in early:
         copy.wait_send()
+    squashed = jnp.tanh(feats[...].astype(F32) / scale)
+    student = (scale * squashed).astype(BF16).astype(F32)
+    slope = 1.0 - squashed * squashed
     for p in (0, 2, 1):
         merge_picks(p)
     for p in (0, 2, 1):
@@ -424,9 +427,7 @@
     both = last_shares(2)
     done = [finish_part(0, *both), finish_part(1, *last_shares(1)), finish_part(2, *both)]
     mean, hit, lse = [jnp.concatenate([done[0][n], done[2][n], done[1][n]], axis=0) for n in range(3)]
-    squashed = jnp.tanh(feats[...].astype(F32) / scale)
-    student = (scale * squashed).astype(BF16).astype(F32)
-    grad_out[...] = (mean - hit) * (1.0 - squashed * squashed)
+    grad_out[...] = (mean - hit) * slope
     column = lse - jnp.sum(student * hit, axis=1, keepdims=True)
     loss_out[...] = jnp.sum(jnp.where(eye, column, 0.0), axis=0, keepdims=True)
 

time: 52.7 us -> 52.8 us (level)
  no operation moved by 1% of the time
where the time goes in v5:
time: 52.8 us; the launch traced here: 52.6 us
  Pallas kernels  49.5 us (94%)
  local copies, waits for them, and re-layouts  2.48 us (5%)
  between operations  0.65 us (1%)
    pallas_call x1, Pallas kernels, body(): pl.pallas_call(kernel, out_shape=(jax.ShapeDtypeStruct((1, 128), F32), ja...  49.5 us
    unnamed x3, local copies, waits for them, and re-layouts  1.97 us

profile of v5, /device:TPU:1, one launch (start us, length us, event | category | flops | bytes accessed | tf_op | source)
XLA Modules:
  0.0 52.6 jit_solution(6957521806671853221)
XLA Ops:
  0.6 49.5 %shard_map.59 = (f32[1,128]{1,0:T(1,128)}, f32[24,256]{1,0:T(8,128)}) custom-call(s32[8]{0:T(128)} %exps_hbm.1, s32[24]{0:T(128)} %tgts_hbm.1, bf16[24,256]{1,0:T(8,128)(2,1)} %feats_hbm.1, bf16[1024,256]{1,0:T(8,128)(2,1)} %cents.1), custom_call_target="tpu_custom_call" | custom-call | tf_op jit(solution)/shard_map/pallas_call | solution.py:445
  50.2 0.0 copy-start
  50.2 0.6 %copy-done = f32[1,128]{1,0:T(1,128)S(1)} copy-done((f32[1,128]{1,0:T(1,128)S(1)}, f32[1,128]{1,0:T(1,128)}, u32[]{:S(2)}) %copy-start) | copy-done | bytes 536
  50.8 0.5 slice_bitcast_fusion
  51.3 1.3 %copy.7 = f32[24,256]{1,0:T(8,128)} copy(f32[24,256]{1,0:T(8,128)} %get-tuple-element.9) | data formatting | bytes 49152
Async XLA Ops:
  50.2 0.6 %copy-start = (f32[1,128]{1,0:T(1,128)S(1)}, f32[1,128]{1,0:T(1,128)}, u32[]{:S(2)}) copy-start(f32[1,128]{1,0:T(1,128)} %get-tuple-element.4) | copy-start | bytes 1540
